TPU v7x, 128 devices: a whole 4x4x4 slice. The times are simulated.
128 devices in a mesh: text: 8 (over y, core), graph: 16 (over x, z).
Axes of the slice: x: 4, y: 4, z: 4, core: 2. Of those that a mesh axis runs over, the one named last changes fastest.
Arguments:
- states: bfloat16 [512, 64, 768], P(('text', 'graph')), may hold values from -6 to 6
- weight_in: bfloat16 [3072, 768], P(('text', 'graph')), may hold values from -0.21875 to 0.21875
- weight_out: bfloat16 [3072, 768], P(('text', 'graph')), may hold values from -0.109375 to 0.109375
- node_table: bfloat16 [131072, 768], P(('text', 'graph')), may hold values from -6 to 6
- adjacency: bfloat16 [1024, 4, 128, 128], P(('text', 'graph')), may hold values from -0.25 to 0.25
- sources: int32 [1024, 4], P(('text', 'graph')), may hold values from 0 to 11
- node_ids: int32 [512], replicated, may hold values from 0 to 131071, as said below
- self_first: bfloat16 [768, 256], replicated, may hold values from -0.21875 to 0.21875
- neigh_first: bfloat16 [768, 256], replicated, may hold values from -0.21875 to 0.21875
- self_second: bfloat16 [256, 256], replicated, may hold values from -0.375 to 0.375
- neigh_second: bfloat16 [256, 256], replicated, may hold values from -0.375 to 0.375
- upstream: bfloat16 [131072, 256], P(('text', 'graph')), may hold values from -6 to 6
Outputs:
- gnn_out: bfloat16 [131072, 256], P(('text', 'graph'))
- table_grad: float32 [131072, 768], P(('text', 'graph'))
- node_grad: float32 [512, 768], P(('text', 'graph'))
- grad_in: float32 [3072, 768], P(('text', 'graph'))
- grad_out: float32 [3072, 768], P(('text', 'graph'))
- grad_self_first: float32 [768, 256], replicated
- grad_neigh_first: float32 [768, 256], replicated
- grad_self_second: float32 [256, 256], replicated
- grad_neigh_second: float32 [256, 256], replicated
Inputs may be any that keep to these rules, and one draw needn't show every extreme that they name: `node_ids`: distinct rows.
All inputs are finite; a program needn't handle non-finite values.
Results may differ from a plain program's by a relative error of at most 0.009.
Values may be sent and summed in bfloat16 or wider, within the bound.
A program may use at most 128 MiB of HBM per device.

v0:
```python
import math

import jax
import jax.numpy as jnp
from jax import lax
from jax.sharding import PartitionSpec as P

BND = 2


precise = lax.Precision.HIGHEST


def passed_along(array, axis, by):
    size = lax.axis_size(axis)
    return lax.ppermute(array, axis, [(i, (i + by) % size) for i in range(size)])


def padded(cells, sides, width):
    for axis, dim in sides:
        count = lax.axis_size(axis)
        head = lax.slice_in_dim(cells, 0, width, axis=dim)
        tail = lax.slice_in_dim(cells, cells.shape[dim] - width, cells.shape[dim], axis=dim)
        cells = jnp.concatenate(
            [
                lax.ppermute(tail, axis, [(i, (i + 1) % count) for i in range(count)]),
                cells,
                lax.ppermute(head, axis, [((i + 1) % count, i) for i in range(count)]),
            ],
            axis=dim,
        )
    return cells


def gelu_value(values):
    return 0.5 * values * (1.0 + jax.scipy.special.erf(values * (1.0 / math.sqrt(2.0))))


def gelu_slope(values):
    normal_cdf = 0.5 * (1.0 + jax.scipy.special.erf(values * (1.0 / math.sqrt(2.0))))
    return normal_cdf + values * jnp.exp(-0.5 * values * values) * (1.0 / math.sqrt(2.0 * math.pi))


def inner_rows(left, right):
    return lax.dot_general(
        left, right, (((0,), (0,)), ((), ())), preferred_element_type=jnp.float32
    )


def times_transposed(left, right):
    return lax.dot_general(
        left, right, (((1,), (1,)), ((), ())), preferred_element_type=jnp.float32
    )


def aggregate_local(extended, adjacency, sources):
    block_rows = adjacency.shape[2]
    wide = extended.shape[1]
    blocks = extended.reshape(-1, block_rows, wide)
    gathered = jnp.take(blocks, sources, axis=0)
    result = jnp.einsum(
        "ntij,ntjw->niw", adjacency.astype(jnp.float32), gathered, precision=precise
    )
    return result.reshape(-1, wide)


def spread_back(values, adjacency, sources, extended_blocks):
    local_blocks = adjacency.shape[0]
    tile_count = adjacency.shape[1]
    block_rows = adjacency.shape[2]
    wide = values.shape[1]
    blocks = values.reshape(local_blocks, block_rows, wide)
    terms = jnp.einsum("ntij,niw->ntjw", adjacency, blocks, preferred_element_type=jnp.float32)
    selector = (
        sources.reshape(1, -1) == jnp.arange(extended_blocks, dtype=jnp.int32)[:, None]
    ).astype(jnp.float32)
    summed = jnp.dot(
        selector, terms.reshape(local_blocks * tile_count, block_rows * wide), precision=precise
    )
    return summed.reshape(extended_blocks * block_rows, wide)


def return_rims(extended, rim_rows, row_count):
    lower_rim = extended[:rim_rows]
    upper_rim = extended[rim_rows + row_count :]
    own_rows = extended[rim_rows : rim_rows + row_count]
    from_next = passed_along(lower_rim, "graph", -1)
    from_prev = passed_along(upper_rim, "graph", 1)
    own_rows = own_rows.at[row_count - rim_rows :].add(from_next)
    own_rows = own_rows.at[:rim_rows].add(from_prev)
    return own_rows


def per_device(
    states,
    weight_in,
    weight_out,
    node_table,
    adjacency,
    sources,
    node_ids,
    self_first,
    neigh_first,
    self_second,
    neigh_second,
    upstream,
):
    node_count = states.shape[0]
    seq_len = states.shape[1]
    model_width = states.shape[2]
    row_count = node_table.shape[0]
    block_rows = adjacency.shape[2]
    local_blocks = row_count // block_rows
    rim_rows = BND * block_rows
    extended_blocks = local_blocks + 2 * BND
    devices_all = lax.axis_size(("text", "graph"))
    wide_states = states.astype(jnp.float32)
    row_mean = jnp.mean(wide_states, axis=-1, keepdims=True)
    centered = wide_states - row_mean
    variance = jnp.mean(centered * centered, axis=-1, keepdims=True)
    normed = (
        (centered * lax.rsqrt(variance + 1e-05))
        .astype(jnp.bfloat16)
        .reshape(node_count * seq_len, model_width)
    )
    before = times_transposed(
        normed, lax.all_gather(weight_in, ("text", "graph"), axis=0, tiled=True)
    )
    active = gelu_value(before).astype(jnp.bfloat16)
    out_full = lax.all_gather(weight_out, ("text", "graph"), axis=0, tiled=True)
    mixed_rows = states.reshape(-1, model_width).astype(jnp.float32) + jnp.dot(
        active, out_full, preferred_element_type=jnp.float32
    )
    embedded = jnp.mean(mixed_rows.reshape(node_count, seq_len, model_width), axis=1).astype(
        jnp.bfloat16
    )
    all_embedded = lax.all_gather(embedded, ("text", "graph"), axis=0, tiled=True)
    row_base = lax.axis_index(("text", "graph")) * row_count
    local_ids = node_ids - row_base
    owned_rows = (local_ids >= 0) & (local_ids < row_count)
    target_rows = jnp.where(owned_rows, local_ids, row_count)
    features = node_table.at[target_rows].set(all_embedded, mode="drop")
    wide_features = padded(features, (("graph", 0),), rim_rows)
    first_proj = jnp.dot(wide_features, neigh_first, preferred_element_type=jnp.float32)
    first_pre = jnp.dot(features, self_first, preferred_element_type=jnp.float32) + aggregate_local(
        first_proj, adjacency, sources
    )
    hidden = gelu_value(first_pre).astype(jnp.bfloat16)
    wide_hidden = padded(hidden, (("graph", 0),), rim_rows)
    second_proj = jnp.dot(wide_hidden, neigh_second, preferred_element_type=jnp.float32)
    second_pre = jnp.dot(hidden, self_second, preferred_element_type=jnp.float32) + aggregate_local(
        second_proj, adjacency, sources
    )
    gnn_out = second_pre.astype(jnp.bfloat16)
    node_scale = 1.0 / math.sqrt(row_count * devices_all)
    back_second = return_rims(
        spread_back(upstream, adjacency, sources, extended_blocks), rim_rows, row_count
    ).astype(jnp.bfloat16)
    local_self_second = inner_rows(hidden, upstream) * node_scale
    local_neigh_second = inner_rows(hidden, back_second) * node_scale
    hidden_grad = times_transposed(upstream, self_second) + times_transposed(
        back_second, neigh_second
    )
    first_grad = (hidden_grad * gelu_slope(first_pre)).astype(jnp.bfloat16)
    back_first = return_rims(
        spread_back(first_grad, adjacency, sources, extended_blocks), rim_rows, row_count
    ).astype(jnp.bfloat16)
    local_self_first = inner_rows(features, first_grad) * node_scale
    local_neigh_first = inner_rows(features, back_first) * node_scale
    table_grad = times_transposed(first_grad, self_first) + times_transposed(
        back_first, neigh_first
    )
    grad_self_first, grad_neigh_first, grad_self_second, grad_neigh_second = lax.psum(
        (local_self_first, local_neigh_first, local_self_second, local_neigh_second),
        ("text", "graph"),
    )
    picked_rows = jnp.take(table_grad, jnp.clip(local_ids, 0, row_count - 1), axis=0)
    picked_rows = jnp.where(owned_rows[:, None], picked_rows, 0.0)
    node_grad = lax.psum_scatter(picked_rows, ("text", "graph"), scatter_dimension=0, tiled=True)
    small_grad = (node_grad / seq_len).astype(jnp.bfloat16)
    grad_nodes = small_grad.shape[0]
    token_grad = jnp.broadcast_to(
        small_grad[:, None, :], (grad_nodes, seq_len, model_width)
    ).reshape(grad_nodes * seq_len, model_width)
    act_grad = times_transposed(token_grad, out_full)
    pre_grad = (act_grad * gelu_slope(before)).astype(jnp.bfloat16)
    adjusted_scale = 1.0 / math.sqrt(node_count * devices_all)
    in_part = inner_rows(pre_grad, normed)
    out_part = inner_rows(active, token_grad)
    summed = lax.psum_scatter(
        jnp.concatenate([in_part, out_part], axis=1) * adjusted_scale,
        ("text", "graph"),
        scatter_dimension=0,
        tiled=True,
    )
    grad_in = summed[:, :model_width]
    grad_out = summed[:, model_width:]
    return (
        gnn_out,
        table_grad,
        node_grad,
        grad_in,
        grad_out,
        grad_self_first,
        grad_neigh_first,
        grad_self_second,
        grad_neigh_second,
    )


def solution(mesh):
    placed = (
        P(("text", "graph"), None, None),
        P(("text", "graph"), None),
        P(("text", "graph"), None),
        P(("text", "graph"), None),
        P(("text", "graph"), None, None, None),
        P(("text", "graph"), None),
        P(),
        P(),
        P(),
        P(),
        P(),
        P(("text", "graph"), None),
    )
    return jax.shard_map(
        per_device,
        mesh=mesh,
        in_specs=placed,
        out_specs=(
            P(("text", "graph"), None),
            P(("text", "graph"), None),
            P(("text", "graph"), None),
            P(("text", "graph"), None),
            P(("text", "graph"), None),
            P(),
            P(),
            P(),
            P(),
        ),
        check_vma=False,
    )
```

profile of v0, /device:TPU:1, one launch (start us, length us, event | category | flops | bytes accessed | tf_op | source)
XLA Modules:
  0.0 757.1 jit_solution(12293614271654792999)
XLA Ops:
  8.9 0.8 fusion.60
  9.7 2.4 copy.61
  12.1 1.6 fusion.43
  13.7 1.0 fusion.55
  14.8 1.9 slice.142
  16.7 6.8 collective-permute-start.4
  23.5 1.9 slice.145
  25.3 1.1 slice.166
  27.3 2.4 slice.139
  29.6 1.9 reshape.198
  32.8 1.3 fusion.59
  34.1 48.0 %all-gather.4.cloned.1.call-done = bf16[3072,768]{1,0:T(8,128)(2,1)} async-done(((bf16[24,768]{1,0:T(8,128)(2,1)}), bf16[3072,768]{1,0:T(8,128)(2,1)}) %all-gather.4.cloned.1.call-update) | async-done | bytes 4718608 | tf_op jit(solution)/shard_map/all_gather | solution.py:127
  82.1 5.5 multiply_convert_fusion
  87.6 62.2 %all-gather.6.cloned.1.call-done = bf16[3072,768]{1,0:T(8,128)(2,1)} async-done(((bf16[24,768]{1,0:T(8,128)(2,1)}), bf16[3072,768]{1,0:T(8,128)(2,1)}) %all-gather.6.cloned.1.call-update) | async-done | bytes 4718608 | tf_op jit(solution)/shard_map/all_gather | solution.py:130
  149.7 3.7 bitcast_reduce_fusion
  153.5 68.0 %all-gather = bf16[128,4,768]{2,1,0:T(4,128)(2,1)} all-gather(bf16[1,4,768]{2,1,0:T(4,128)(2,1)S(1)} %fusion.44), channel_id=1, replica_groups=mesh['text'=8,'graph'=16] {'text','graph'}, dimensions={0}, use_global_device_ids=true | all-gather | bytes 792576 | tf_op jit(solution)/shard_map/all_gather | solution.py:137
  221.5 2.3 reshape.243
  223.8 4.1 scatter_fusion
  228.5 4.3 collective-permute-start.1
  232.8 1.7 add_dynamic-update-slice_fusion.1
  234.4 1.8 fusion.37
  236.2 5.1 collective-permute-done
  241.3 1.9 fusion.9
  243.3 4.2 gather_fusion.1
  247.5 4.2 fusion.2
  253.8 1.5 convolution_multiply_fusion.2
  255.3 2.3 fusion.61
  257.6 2.7 convolution_bitcast_fusion
  260.3 5.5 copy.62
  265.8 3.8 fusion.42
  269.7 1.3 copy-done.4
  271.0 1.0 fusion.54
  272.0 1.9 slice.150
  273.9 4.5 collective-permute-start.6
  278.4 2.3 convolution_multiply_fusion.3
  280.6 1.9 slice.153
  282.5 2.1 convolution_multiply_fusion.4
  284.6 2.7 slice.171
  287.3 2.4 slice.147
  289.6 1.9 reshape.201
  291.5 1.8 add_dynamic-update-slice_fusion
  293.3 1.9 fusion.36
  295.2 2.8 convolution_multiply_fusion.1
  298.0 2.3 convolution_add_fusion
  300.3 5.1 gather_fusion
  305.4 2.9 select_select_fusion
  308.4 154.8 %all-reduce.4.cloned.1.call-done = (f32[512,768]{1,0:T(8,128)}, f32[768,256]{1,0:T(8,128)}, f32[768,256]{1,0:T(8,128)}, f32[256,256]{1,0:T(8,128)}, f32[256,256]{1,0:T(8,128)}) async-done(((f32[512,768]{1,0:T(8,128)}, f32[768,256]{1,0:T(8,128)}, f32[768,256]{1,0:T(8,128)}, f32[256,256]{1,0:T(8,128)}, f32[256,256]{1,0:T(8,128)}), (f32[512,768]{1,0:T(8,128)}, f32[768,256]{1,0:T(8,128)}, f32[768,256]{1,0:T(8,128)}, ...) | async-done | bytes 3670032
  463.2 1.3 multiply_convert_fusion.3
  464.6 5.1 fusion.62
  469.7 7.7 %fusion.19 = f32[3072,768]{0,1:T(8,128)} fusion(bf16[256,768]{1,0:T(8,128)(2,1)S(1)} %bitcast.92, bf16[256,768]{1,0:T(8,128)(2,1)} %bitcast.94, bf16[3072,768]{1,0:T(8,128)(2,1)} %all-gather.6.cloned.1.call-done, f32[256,3072]{1,0:T(8,128)} %get-tuple-element.108), kind=kOutput, calls=%fused_computation.29 | convolution fusion | flops 2423783424 | bytes 18087936 | tf_op jit(solution)/shard_map/dot_general | solution.py:45
  477.4 14.6 %maximum_multiply_fusion = f32[3072,1536]{0,1:T(8,128)} fusion(f32[3072,768]{0,1:T(8,128)} %fusion.62, f32[3072,768]{0,1:T(8,128)} %fusion.19), kind=kLoop, calls=%fused_computation.4 | loop fusion | flops 9437184 | bytes 37748736 | tf_op jit(solution)/shard_map/mul | solution.py:191
  492.0 18.6 %copy.57 = f32[3072,1536]{1,0:T(8,128)} copy(f32[3072,1536]{0,1:T(8,128)} %maximum_multiply_fusion) | data formatting | bytes 37748736
  510.7 0.8 collective-permute-start.2
  511.5 4.0 collective-permute-start.3
  515.6 2.7 collective-permute-done.2
  518.7 2.9 gather_fusion.2
  521.6 4.3 fusion
  525.9 1.1 fusion.25
  527.0 217.5 %reduce-scatter.4.cloned.1.call-done = f32[24,1536]{1,0:T(8,128)} async-done(((f32[3072,1536]{1,0:T(8,128)}), f32[24,1536]{1,0:T(8,128)}) %reduce-scatter.4.cloned.1.call-update) | async-done | bytes 147472
  744.5 1.6 fusion.58
  746.1 0.9 copy.76
  746.9 0.9 copy.77
  747.8 1.7 copy.78
  749.5 0.7 copy.79
  (101 shorter events, 7.0 us)
Async XLA Ops:
  7.2 1.7 copy-start
  7.2 1.6 copy-start.25
  7.2 1.7 copy-start.12
  7.2 74.9 %all-gather.4.cloned.1.call-start = ((), (), s32[]{:S(2)}) async-start(), calls=%async_computation.1 | async-start | bytes 4755456 | tf_op jit(solution)/shard_map/all_gather | solution.py:127
  7.9 141.8 %all-gather.6.cloned.1.call-start = ((), (), s32[]{:S(2)}) async-start(), calls=%async_computation.2 | async-start | bytes 4755456 | tf_op jit(solution)/shard_map/all_gather | solution.py:130
  8.7 454.5 %all-reduce.4.cloned.1.call-start = ((), (), s32[]{:S(2)}) async-start(), calls=%async_computation.4 | async-start | bytes 7340032
  8.9 3.2 copy-start.27
  14.8 16.8 %copy-start.26 = (s32[512]{0:T(512)S(1)}, s32[512]{0:T(512)}, u32[]{:S(2)}) copy-start(s32[512]{0:T(512)} %param.28) | copy-start | bytes 6148
  14.8 17.4 %copy-start.10 = (bf16[4,64,768]{2,1,0:T(8,128)(2,1)S(1)}, bf16[4,64,768]{2,1,0:T(8,128)(2,1)}, u32[]{:S(2)}) copy-start(bf16[4,64,768]{2,1,0:T(8,128)(2,1)} %param.22) | copy-start | bytes 1179652
  16.7 216.1 %collective-permute-start.4 = (f32[256,256]{1,0:T(8,128)}, f32[256,256]{1,0:T(8,128)}, u32[]{:S(2)}, u32[]{:S(2)}) collective-permute-start(f32[256,256]{1,0:T(8,128)} %slice.142), channel_id=1, source_target_pairs={{0,15},{1,0},{2,1},{3,2},{4,3},{5,4},{6,5},{7,6},{8,7},{9,8},{10,9... | collective-permute-start | bytes 786440 | tf_op jit(solution)/shard_map/ppermute | solution.py:16
  25.3 209.1 %collective-permute-start.5 = (f32[256,256]{1,0:T(8,128)}, f32[256,256]{1,0:T(8,128)}, u32[]{:S(2)}, u32[]{:S(2)}) collective-permute-start(f32[256,256]{1,0:T(8,128)} %slice.145), channel_id=1, source_target_pairs={{0,1},{1,2},{2,3},{3,4},{4,5},{5,6},{6,7},{7,8},{8,9},{9,10},{10,1... | collective-permute-start | bytes 786440 | tf_op jit(solution)/shard_map/ppermute | solution.py:16
  26.4 6.1 copy-start.11
  26.4 6.3 copy-start.13
  26.4 6.3 copy-start.18
  87.6 62.2 %copy-start.5 = (bf16[256,3072]{1,0:T(8,128)(2,1)}, bf16[256,3072]{1,0:T(8,128)(2,1)S(1)}, u32[]{:S(2)}) copy-start(bf16[256,3072]{1,0:T(8,128)(2,1)S(1)} %get-tuple-element.107) | copy-start | bytes 4718596
  153.5 70.3 %copy-start.1 = (bf16[1024,768]{1,0:T(8,128)(2,1)S(1)}, bf16[1024,768]{1,0:T(8,128)(2,1)}, u32[]{:S(2)}) copy-start(bf16[1024,768]{1,0:T(8,128)(2,1)} %param.25) | copy-start | bytes 4718596
  223.7 9.0 %copy-start.15 = (f32[256,256]{1,0:T(8,128)S(1)}, f32[256,256]{1,0:T(8,128)}, u32[]{:S(2)}) copy-start(f32[256,256]{1,0:T(8,128)} %reshape.198) | copy-start | bytes 786436
  227.8 13.5 %copy-start.22 = (bf16[768,256]{1,0:T(8,128)(2,1)S(1)}, bf16[768,256]{1,0:T(8,128)(2,1)}, u32[]{:S(2)}) copy-start(bf16[768,256]{1,0:T(8,128)(2,1)} %param.30) | copy-start | bytes 1179652
  227.9 13.4 %collective-permute-start = (bf16[256,768]{1,0:T(8,128)(2,1)S(1)}, bf16[256,768]{1,0:T(8,128)(2,1)S(1)}, u32[]{:S(2)}, u32[]{:S(2)}) collective-permute-start(bf16[256,768]{1,0:T(8,128)(2,1)S(1)} %get-tuple-element.100), channel_id=1, source_target_pairs={{0,1},{1,2},{2,3},{3,4},{4,5},{5,6},{6,7},{7,8},{8,9},{9,10},{10,1... | collective-permute-start | bytes 1179656 | tf_op jit(solution)/shard_map/ppermute | solution.py:26
  228.5 12.8 %collective-permute-start.1 = (bf16[256,768]{1,0:T(8,128)(2,1)S(1)}, bf16[256,768]{1,0:T(8,128)(2,1)S(1)}, u32[]{:S(2)}, u32[]{:S(2)}) collective-permute-start(bf16[256,768]{1,0:T(8,128)(2,1)S(1)} %get-tuple-element.101), channel_id=1, source_target_pairs={{1,0},{2,1},{3,2},{4,3},{5,4},{6,5},{7,6},{8,7},{9,8},{10,9},{11,1... | collective-permute-start | bytes 1179656 | tf_op jit(solution)/shard_map/ppermute | solution.py:28
  243.3 4.2 copy-start.29
  247.5 4.2 copy-start.14
  251.6 1.2 copy-start.3
  251.6 1.5 copy-start.8
  251.6 1.5 copy-start.20
  260.3 5.5 copy-start.28
  269.6 1.4 copy-start.4
  273.9 17.6 %collective-permute-start.6 = (f32[256,256]{1,0:T(8,128)}, f32[256,256]{1,0:T(8,128)}, u32[]{:S(2)}, u32[]{:S(2)}) collective-permute-start(f32[256,256]{1,0:T(8,128)} %slice.150), channel_id=1, source_target_pairs={{0,15},{1,0},{2,1},{3,2},{4,3},{5,4},{6,5},{7,6},{8,7},{9,8},{10,9... | collective-permute-start | bytes 786440 | tf_op jit(solution)/shard_map/ppermute | solution.py:16
  282.5 10.8 %collective-permute-start.7 = (f32[256,256]{1,0:T(8,128)}, f32[256,256]{1,0:T(8,128)}, u32[]{:S(2)}, u32[]{:S(2)}) collective-permute-start(f32[256,256]{1,0:T(8,128)} %slice.153), channel_id=1, source_target_pairs={{0,1},{1,2},{2,3},{3,4},{4,5},{5,6},{6,7},{7,8},{8,9},{9,10},{10,1... | collective-permute-start | bytes 786440 | tf_op jit(solution)/shard_map/ppermute | solution.py:16
  293.3 4.7 copy-start.2
  293.3 4.7 copy-start.23
  295.2 2.8 copy-start.7
  300.3 5.1 copy-start.30
  305.4 159.2 %copy-start.6 = (bf16[256,3072]{1,0:T(8,128)(2,1)S(1)}, bf16[256,3072]{1,0:T(8,128)(2,1)}, u32[]{:S(2)}) copy-start(bf16[256,3072]{1,0:T(8,128)(2,1)} %copy-done.5) | copy-start | bytes 4718596
  308.4 436.1 %reduce-scatter.4.cloned.1.call-start = ((), (), s32[]{:S(2)}) async-start(), calls=%async_computation.3 | async-start | bytes 19021824
  464.6 5.1 copy-start.9
  510.7 7.7 %copy-start.21 = (bf16[256,256]{1,0:T(8,128)(2,1)S(1)}, bf16[256,256]{1,0:T(8,128)(2,1)}, u32[]{:S(2)}) copy-start(bf16[256,256]{1,0:T(8,128)(2,1)} %param.32) | copy-start | bytes 393220
  510.7 7.6 %collective-permute-start.2 = (bf16[256,256]{1,0:T(8,128)(2,1)S(1)}, bf16[256,256]{1,0:T(8,128)(2,1)S(1)}, u32[]{:S(2)}, u32[]{:S(2)}) collective-permute-start(bf16[256,256]{1,0:T(8,128)(2,1)S(1)} %get-tuple-element.102), channel_id=1, source_target_pairs={{0,1},{1,2},{2,3},{3,4},{4,5},{5,6},{6,7},{7,8},{8,9},{9,10},{10,1... | collective-permute-start | bytes 393224 | tf_op jit(solution)/shard_map/ppermute | solution.py:26
  511.5 6.8 collective-permute-start.3
  521.5 4.3 copy-start.19
  521.5 224.5 %copy-start.17 = (f32[768,256]{1,0:T(8,128)S(1)}, f32[768,256]{1,0:T(8,128)}, u32[]{:S(2)}) copy-start(f32[768,256]{1,0:T(8,128)} %get-tuple-element.116) | copy-start | bytes 2359300
  525.9 221.1 %copy-start.16 = (f32[768,256]{1,0:T(8,128)S(1)}, f32[768,256]{1,0:T(8,128)}, u32[]{:S(2)}) copy-start(f32[768,256]{1,0:T(8,128)} %get-tuple-element.117) | copy-start | bytes 2359300
  525.9 223.6 %copy-start.24 = (f32[256,256]{1,0:T(8,128)S(1)}, f32[256,256]{1,0:T(8,128)}, u32[]{:S(2)}) copy-start(f32[256,256]{1,0:T(8,128)} %get-tuple-element.119) | copy-start | bytes 786436
Sparse Core Ops, SparseCore 0:
  11.1 70.8 all-gather.3
  85.2 64.5 all-gather.5
  308.5 154.6 all-reduce.3
  510.8 233.6 reduce-scatter.3
where the time goes:
time: 767 us; the launch traced here: 757 us
  waiting for transfers between devices  492 us (64%)
  local copies, waits for them, and re-layouts  76.1 us (10%)
  blocking collectives  68 us (9%)
  matrix products  58.5 us (8%)
  other arithmetic  27.2 us (4%)
  starting transfers between devices  21.1 us (3%)
  between operations  14.5 us (2%)
    unnamed x6, waiting for transfers between devices  374 us
    all_gather x1, blocking collectives, per_device(): lax.all_gather(embedded, ('text', 'graph'), axis=0, tiled=True)  68 us
    all_gather x1, waiting for transfers between devices, per_device(): out_full = lax.all_gather(weight_out, ('text', 'graph'), axis=0, tiled=True)  62.2 us
    all_gather x1, waiting for transfers between devices, per_device(): lax.all_gather(weight_in, ('text', 'graph'), axis=0, tiled=True)  48 us
    unnamed x71, local copies, waits for them, and re-layouts  35.4 us
    dot_general x6, matrix products, inner_rows(): lax.dot_general(left, right, (((0,), (0,)), ((), ())), preferred_element_...  21.5 us
  transfers between devices with their start and end apart: 12, of which 6 were waited for; matrix products, arithmetic and copies ran while one was open for 8% of the time, Pallas kernels for 0%

commit v1 on v0

v1 whole, which is shorter than its diff:
```python
import math
from types import SimpleNamespace

import jax
import jax.numpy as jnp
from jax import lax
from jax.experimental import pallas as pl
from jax.experimental.pallas import tpu as pltpu
from jax.sharding import PartitionSpec as P

MESH = pl.DeviceIdType.MESH
F32 = jnp.float32
BF16 = jnp.bfloat16

D = 768
FFH = 3072
HID = 256
SEQ = 64
ROWS = 1024
RIM = 256
EXT = ROWS + 2 * RIM
NFT = 512
NG = 16
NT = 8
CHUNK = FFH // NT
OWN = FFH // (NT * NG)
NODE_SCALE = 1.0 / math.sqrt(131072)
TEXT_SCALE = 1.0 / math.sqrt(NFT)

INPUTS = (
    "states", "w_in", "w_out", "table", "adj", "src", "ids",
    "sf", "nf", "ss", "ns", "ups",
)
OUTPUTS = {
    "gnn": ((ROWS, HID), BF16),
    "tgrad": ((ROWS, D), F32),
    "ngrad": ((4, D), F32),
    "gin": ((OWN, D), F32),
    "gout": ((OWN, D), F32),
    "gsf": ((D, HID), F32),
    "gnf": ((D, HID), F32),
    "gss": ((HID, HID), F32),
    "gns": ((HID, HID), F32),
}
SCRATCH = {
    "wpack": ((NG, 2 * OWN, D), BF16),
    "wide_in": ((CHUNK, D), F32),
    "wide_out": ((CHUNK, D), F32),
    "wi": ((CHUNK, D), BF16),
    "wo": ((CHUNK, D), BF16),
    "normed": ((NT, 256, D), BF16),
    "smean": ((8, D), F32),
    "before": ((256, CHUNK), F32),
    "slope": ((NT, 256, CHUNK), F32),
    "asum": ((32, CHUNK), F32),
    "part": ((32, D), F32),
    "part2": ((2, 16, D), F32),
    "pairin": ((16, D), F32),
    "yemb": ((4, 16, D), BF16),
    "emb": ((2, NG, 16, D), BF16),
    "oh": ((EXT, NFT), BF16),
    "oht": ((NFT, EXT), BF16),
    "keep": ((EXT, 1), F32),
    "e": ((ROWS, EXT), BF16),
    "et": ((EXT, ROWS), BF16),
    "b2": ((EXT, HID), F32),
    "b2out": ((2, RIM, HID), BF16),
    "b2in": ((2, RIM, HID), BF16),
    "back2": ((ROWS, HID), BF16),
    "hg": ((ROWS, HID), F32),
    "tself": ((ROWS, HID), F32),
    "tn": ((EXT, HID), BF16),
    "pn": ((EXT, HID), BF16),
    "embproj": ((NFT, 2 * HID), BF16),
    "hid": ((EXT, HID), BF16),
    "proj2": ((EXT, HID), BF16),
    "fb": ((ROWS, 2 * HID), BF16),
    "b1": ((EXT, HID), F32),
    "b1b": ((EXT, HID), BF16),
    "b1in": ((2, RIM, HID), BF16),
    "feat": ((ROWS, D), BF16),
    "wg": ((2, 4, NG, 16, HID), BF16),
    "wgin": ((4, NG, 16, HID), BF16),
    "wg1": ((4, NG, 16, HID), BF16),
    "wgy": ((4, NG, 16, HID), BF16),
    "wg2": ((NG, 16, HID), BF16),
    "wgg": ((NG, 16, HID), BF16),
    "wgall": ((2, 4, NG, 16, HID), BF16),
    "pick": ((2, NG, 16, 2 * HID), BF16),
    "pickin": ((NG, 16, 2 * HID), BF16),
    "pick1": ((NG, 16, 2 * HID), BF16),
    "pickg": ((NG, 16, 2 * HID), BF16),
    "picky": ((4, 16, 2 * HID), BF16),
    "pickall": ((2, 16, 2 * HID), BF16),
    "nodeg": ((32, D), F32),
    "act": ((32, CHUNK), F32),
    "pre": ((NT, 256, CHUNK), BF16),
    "gfull": ((2, CHUNK, D), F32),
    "gpack": ((NG, 2 * OWN, D), BF16),
    "grecv": ((NG, 2 * OWN, D), BF16),
}
SEMS = {
    "w": 16, "st": 9, "rim": 8, "pair": 1, "ye": 4, "eg": 16, "es": 16,
    "pk": 1, "pg": 16, "py": 4, "ps": 1,
    "a1": 1, "a2": 4, "a3": 16, "a4": 16, "a5": 4, "a6": 1, "gr": 16,
}


def dot(a, b):
    return jnp.dot(a, b, preferred_element_type=F32)


def dot_nt(a, b):
    return lax.dot_general(a, b, (((1,), (1,)), ((), ())), preferred_element_type=F32)


def dot_tn(a, b):
    return lax.dot_general(a, b, (((0,), (0,)), ((), ())), preferred_element_type=F32)


def gelu_pair(v):
    cdf = 0.5 * (1.0 + lax.erf(v * (1.0 / math.sqrt(2.0))))
    return v * cdf, cdf + v * jnp.exp(-0.5 * v * v) * (1.0 / math.sqrt(2.0 * math.pi))


def split(v):
    high = v.astype(BF16)
    return high, (v - high.astype(F32)).astype(BF16)


def body(*refs):
    names = list(INPUTS) + list(OUTPUTS) + list(SCRATCH)
    r = SimpleNamespace(**dict(zip(names, refs)))
    sems = {}
    at = len(names)
    for name in SEMS:
        sems[name] = (refs[at], refs[at + 1])
        at += 2

    t = lax.axis_index("text")
    g = lax.axis_index("graph")
    c = lax.rem(t, 2)
    y = lax.div(t, 2)
    sib = t + 1 - 2 * c

    def at_y(step):
        return lax.rem(y + step, 4) * 2 + c

    up, opp, down = at_y(1), at_y(2), at_y(3)
    ahead = lax.rem(g + 1, NG)
    behind = lax.rem(g + NG - 1, NG)
    pending = []

    def send(src, dst, kind, tag, to, start=True):
        copy = pltpu.make_async_remote_copy(
            src_ref=src, dst_ref=dst, send_sem=sems[kind][0].at[tag],
            recv_sem=sems[kind][1].at[tag], device_id=to, device_id_type=MESH,
        )
        if start:
            copy.start()
            pending.append(copy)
        return copy

    def arrived(dst, kind, tag):
        send(dst, dst, kind, tag, (sib, g), start=False).wait_recv()

    def each_peer(fn):
        def step(k, carry):
            fn(k, lax.rem(g + k, NG), lax.rem(g + NG - k, NG))
            return carry

        lax.fori_loop(1, NG, step, 0)

    def scatter(src_of, dst, kind):
        def one(k, to, source):
            pltpu.make_async_remote_copy(
                src_ref=src_of(to), dst_ref=dst.at[g], send_sem=sems[kind][0].at[k],
                recv_sem=sems[kind][1].at[k], device_id=(t, to), device_id_type=MESH,
            ).start()

        each_peer(one)

    def scatter_wait(dst, kind):
        each_peer(lambda k, to, source: arrived(dst.at[source], kind, k))

    def scatter_sent(src, kind):
        def one(k, to, source):
            send(src, src, kind, k, (t, to), start=False).wait_send()

        each_peer(one)

    barrier = pltpu.get_barrier_semaphore()

    def greet(to):
        pl.semaphore_signal(barrier, inc=1, device_id=to, device_id_type=MESH)

    for peer in (sib, up, opp, down):
        greet((peer, g))
    each_peer(lambda k, to, source: greet((t, to)))
    pl.semaphore_wait(barrier, 19)

    both = jnp.concatenate([r.w_in[...].astype(F32), r.w_out[...].astype(F32)], axis=0)
    r.wpack[g] = both.astype(BF16)
    scatter(lambda to: r.wpack.at[g], r.wpack, "w")

    for i in range(4):
        x = r.states[i * SEQ : (i + 1) * SEQ, :].astype(F32)
        r.smean[i : i + 1, :] = jnp.sum(x, axis=0, keepdims=True) * (1.0 / SEQ)
        mean = jnp.mean(x, axis=1, keepdims=True)
        centered = x - mean
        var = jnp.mean(centered * centered, axis=1, keepdims=True)
        r.normed[t, i * SEQ : (i + 1) * SEQ, :] = (centered * lax.rsqrt(var + 1e-05)).astype(BF16)
    mine = r.normed.at[t]
    send(mine, mine, "st", 0, (sib, g))
    send(mine, mine, "st", 1, (up, g))
    send(mine, mine, "st", 2, (down, g))

    for i in (0, 3, 1, 2):
        rows = slice(i * 256, (i + 1) * 256)
        x = r.table[rows, :]
        r.tn[RIM + i * 256 : RIM + (i + 1) * 256, :] = dot(x, r.nf[...]).astype(BF16)
        r.tself[rows, :] = dot(x, r.sf[...])
        if i == 3:
            send(r.tn.at[RIM : 2 * RIM], r.tn.at[RIM + ROWS :], "rim", 0, (t, behind))
            send(r.tn.at[ROWS : ROWS + RIM], r.tn.at[:RIM], "rim", 1, (t, ahead))

    def tiles(b, carry):
        rows = pl.ds(pl.multiple_of(b * 128, 128), 128)
        plain = [r.adj[b * 4 + k] for k in range(4)]
        turned = [p.astype(F32).T.astype(BF16) for p in plain]
        for s in range(12):
            own = jnp.zeros((128, 128), BF16)
            other = jnp.zeros((128, 128), BF16)
            for k in range(4):
                hit = r.src[b, k] == s
                own = own + jnp.where(hit, plain[k], jnp.zeros_like(plain[k]))
                other = other + jnp.where(hit, turned[k], jnp.zeros_like(turned[k]))
            r.e[rows, s * 128 : (s + 1) * 128] = own
            r.et[s * 128 : (s + 1) * 128, rows] = other
        return carry

    lax.fori_loop(0, 8, tiles, 0)

    for i in (0, 5, 1, 2, 3, 4):
        rows = slice(i * 256, (i + 1) * 256)
        r.b2[rows, :] = dot(r.et[rows, :], r.ups[...])
        if i == 5:
            r.b2out[0] = r.b2[:RIM, :].astype(BF16)
            r.b2out[1] = r.b2[RIM + ROWS :, :].astype(BF16)
            send(r.b2out.at[0], r.b2in.at[1], "rim", 2, (t, behind))
            send(r.b2out.at[1], r.b2in.at[0], "rim", 3, (t, ahead))

    row = lax.broadcasted_iota(jnp.int32, (NFT, NFT), 0)
    col = lax.broadcasted_iota(jnp.int32, (NFT, NFT), 1)
    wanted = (col & 256) + ((col >> 2) & 3) * 64 + ((col >> 4) & 15) * 4 + (col & 3)
    moved = jnp.where(row == wanted, 1.0, 0.0).astype(BF16)
    ids = jnp.broadcast_to(r.ids[...], (8, NFT))
    pieces = [((ids >> shift) & 63).astype(F32).astype(BF16) for shift in (0, 6, 12)]
    low, middle, high = [dot(p, moved) for p in pieces]
    spot = low + 64.0 * middle + 4096.0 * high
    spot_row = spot[:1, :]
    spot_col = jnp.broadcast_to(spot_row, (128, NFT)).T
    device = t * NG + g
    starts = [(t * NG + behind) * ROWS + 768 + e * 128 for e in range(2)]
    starts += [device * ROWS + e * 128 for e in range(8)]
    starts += [(t * NG + ahead) * ROWS + e * 128 for e in range(2)]
    for e in range(12):
        start = starts[e].astype(F32)
        down_rows = lax.broadcasted_iota(jnp.int32, (128, NFT), 0).astype(F32) + start
        hit = jnp.where(down_rows == spot_row, 1.0, 0.0)
        r.oh[e * 128 : (e + 1) * 128, :] = hit.astype(BF16)
        r.keep[e * 128 : (e + 1) * 128, :] = 1.0 - jnp.sum(hit, axis=1, keepdims=True)
        across = lax.broadcasted_iota(jnp.int32, (NFT, 128), 1).astype(F32) + start
        r.oht[:, e * 128 : (e + 1) * 128] = jnp.where(across == spot_col, 1.0, 0.0).astype(BF16)

    scatter_wait(r.wpack, "w")

    def unpack(k, carry):
        block = r.wpack[k].astype(F32)
        rows = pl.ds(pl.multiple_of(k * OWN, 8), OWN)
        r.wide_in[rows, :] = block[:OWN]
        r.wide_out[rows, :] = block[OWN:]
        return carry

    lax.fori_loop(0, NG, unpack, 0)
    r.wi[...] = r.wide_in[...].astype(BF16)
    r.wo[...] = r.wide_out[...].astype(BF16)

    def encode(slot):
        r.before[...] = dot_nt(r.normed[slot], r.wi[...])

        def node(i, carry):
            rows = pl.ds(pl.multiple_of(i * SEQ, SEQ), SEQ)
            value, slope = gelu_pair(r.before[rows, :])
            r.slope[slot, rows, :] = slope
            r.asum[pl.ds(slot * 4 + i, 1), :] = jnp.sum(value, axis=0, keepdims=True)
            return carry

        lax.fori_loop(0, 4, node, 0)

    def fellow(slot):
        return slot + 1 - 2 * c

    encode(t)
    from_down, from_up, far = r.normed.at[down], r.normed.at[up], r.normed.at[opp]
    arrived(from_down, "st", 1)
    send(from_down.at[:128], from_down.at[:128], "st", 3, (up, g))
    send(from_down, from_down, "st", 5, (sib, g))
    arrived(from_up, "st", 2)
    send(from_up.at[128:], from_up.at[128:], "st", 4, (down, g))
    send(from_up, from_up, "st", 6, (sib, g))
    arrived(r.normed.at[sib], "st", 0)
    encode(sib)
    encode(down)
    encode(up)
    arrived(far.at[:128], "st", 3)
    send(far.at[:128], far.at[:128], "st", 7, (sib, g))
    arrived(far.at[128:], "st", 4)
    send(far.at[128:], far.at[128:], "st", 8, (sib, g))
    arrived(r.normed.at[fellow(down)], "st", 5)
    encode(fellow(down))
    arrived(r.normed.at[fellow(up)], "st", 6)
    encode(fellow(up))
    encode(opp)
    far_pair = r.normed.at[fellow(opp)]
    arrived(far_pair.at[:128], "st", 7)
    arrived(far_pair.at[128:], "st", 8)
    encode(fellow(opp))

    a_high, a_low = split(r.asum[...] * (1.0 / SEQ))
    r.part[...] = dot(a_high, r.wo[...]) + dot(a_low, r.wo[...])
    for i in range(4):
        spot_rows = pl.ds(t * 4 + i, 1)
        r.part[spot_rows, :] = r.part[spot_rows, :] + r.smean[i : i + 1, :]
    r.part2[0] = r.part[:16, :]
    r.part2[1] = r.part[16:, :]
    send(r.part2.at[1 - c], r.pairin, "pair", 0, (sib, g))
    arrived(r.pairin, "pair", 0)
    r.yemb[y] = (r.part2[c] + r.pairin[...]).astype(BF16)
    for step, peer in ((1, up), (2, opp), (3, down)):
        send(r.yemb.at[y], r.yemb.at[y], "ye", step, (peer, g))
    for step in (1, 2, 3):
        arrived(r.yemb.at[lax.rem(y + 4 - step, 4)], "ye", step)
    total = r.yemb[0].astype(F32) + r.yemb[1].astype(F32)
    total = total + r.yemb[2].astype(F32) + r.yemb[3].astype(F32)
    r.emb[c, g] = total.astype(BF16)

    def emb_out(k, to, source):
        ref = r.emb.at[c, g]
        send(ref, ref, "eg", k, (t, to), start=False).start()

    each_peer(emb_out)
    own_emb = r.emb.at[c, g]
    send(own_emb, own_emb, "es", 0, (sib, g))

    arrived(r.b2in.at[0], "rim", 3)
    arrived(r.b2in.at[1], "rim", 2)
    r.b2[RIM : 2 * RIM, :] = r.b2[RIM : 2 * RIM, :] + r.b2in[0].astype(F32)
    r.b2[ROWS : ROWS + RIM, :] = r.b2[ROWS : ROWS + RIM, :] + r.b2in[1].astype(F32)
    r.back2[...] = r.b2[RIM : RIM + ROWS, :].astype(BF16)
    for i in range(4):
        rows = slice(i * 256, (i + 1) * 256)
        r.hg[rows, :] = dot_nt(r.ups[rows, :], r.ss[...]) + dot_nt(r.back2[rows, :], r.ns[...])
    arrived(r.tn.at[RIM + ROWS :], "rim", 0)
    arrived(r.tn.at[:RIM], "rim", 1)

    def emb_on(k, to, source):
        ref = r.emb.at[c, source]
        arrived(ref, "eg", k)
        send(ref, ref, "es", k, (sib, g), start=False).start()

    each_peer(emb_on)
    arrived(r.emb.at[1 - c, g], "es", 0)
    each_peer(lambda k, to, source: arrived(r.emb.at[1 - c, source], "es", k))

    emb_all = r.emb[...].reshape(NFT, D)
    r.embproj[:, :HID] = dot(emb_all, r.sf[...]).astype(BF16)
    r.embproj[:, HID:] = dot(emb_all, r.nf[...]).astype(BF16)
    for i in range(6):
        rows = slice(i * 256, (i + 1) * 256)
        new = dot(r.oh[rows, :], r.embproj[:, HID:])
        r.pn[rows, :] = (r.tn[rows, :].astype(F32) * r.keep[rows, :] + new).astype(BF16)

    for i in range(4):
        rows = slice(i * 256, (i + 1) * 256)
        ext = slice(RIM + i * 256, RIM + (i + 1) * 256)
        pre = r.tself[rows, :] * r.keep[ext, :] + dot(r.oh[ext, :], r.embproj[:, :HID])
        pre = pre + dot(r.e[rows, :], r.pn[...])
        value, slope = gelu_pair(pre)
        r.hid[ext, :] = value.astype(BF16)
        r.fb[rows, :HID] = (r.hg[rows, :] * slope).astype(BF16)
    send(r.hid.at[RIM : 2 * RIM], r.hid.at[RIM + ROWS :], "rim", 4, (t, behind))
    send(r.hid.at[ROWS : ROWS + RIM], r.hid.at[:RIM], "rim", 5, (t, ahead))
    for i in (0, 5, 1, 2, 3, 4):
        rows = slice(i * 256, (i + 1) * 256)
        term = dot(r.et[rows, :], r.fb[:, :HID])
        r.b1[rows, :] = term
        r.b1b[rows, :] = term.astype(BF16)
    send(r.b1b.at[:RIM], r.b1in.at[1], "rim", 6, (t, behind))
    send(r.b1b.at[RIM + ROWS :], r.b1in.at[0], "rim", 7, (t, ahead))

    for i in range(2):
        rows = slice(i * 256, (i + 1) * 256)
        first = dot(r.oht[rows, RIM : RIM + ROWS], r.fb[:, :HID]).astype(BF16)
        back = dot(r.oht[rows, :], r.b1b[...]).astype(BF16)
        r.pick[i, :, :, :HID] = first.reshape(NG, 16, HID)
        r.pick[i, :, :, HID:] = back.reshape(NG, 16, HID)
    send(r.pick.at[1 - c], r.pickin, "pk", 0, (sib, g))

    def features(i):
        rows = slice(i * 256, (i + 1) * 256)
        ext = slice(RIM + i * 256, RIM + (i + 1) * 256)
        old = r.table[rows, :].astype(F32) * r.keep[ext, :]
        r.feat[rows, :] = (old + dot(r.oh[ext, :], emb_all)).astype(BF16)

    features(0)
    features(1)
    arrived(r.pickin, "pk", 0)
    r.pick1[...] = (r.pick[c].astype(F32) + r.pickin[...].astype(F32)).astype(BF16)
    r.pickg[g] = r.pick1[g]
    scatter(lambda to: r.pick1.at[to], r.pickg, "pg")
    features(2)
    features(3)

    arrived(r.b1in.at[0], "rim", 7)
    arrived(r.b1in.at[1], "rim", 6)
    r.b1[RIM : 2 * RIM, :] = r.b1[RIM : 2 * RIM, :] + r.b1in[0].astype(F32)
    r.b1[ROWS : ROWS + RIM, :] = r.b1[ROWS : ROWS + RIM, :] + r.b1in[1].astype(F32)
    r.fb[:, HID:] = r.b1[RIM : RIM + ROWS, :].astype(BF16)

    for side in range(2):
        cols = slice(side * HID, (side + 1) * HID)
        for q in range(3):
            term = dot_tn(r.feat[:, q * 256 : (q + 1) * 256], r.fb[:, cols])
            r.wg[side, q] = (term * NODE_SCALE).astype(BF16).reshape(NG, 16, HID)
    hidden = r.hid[RIM : RIM + ROWS, :]
    r.wg[0, 3] = (dot_tn(hidden, r.ups[...]) * NODE_SCALE).astype(BF16).reshape(NG, 16, HID)
    r.wg[1, 3] = (dot_tn(hidden, r.back2[...]) * NODE_SCALE).astype(BF16).reshape(NG, 16, HID)
    send(r.wg.at[1 - c], r.wgin, "a1", 0, (sib, g))

    scatter_wait(r.pickg, "pg")
    mixed = r.pickg[0].astype(F32)
    for k in range(1, NG):
        mixed = mixed + r.pickg[k].astype(F32)
    r.picky[y] = mixed.astype(BF16)
    for step, peer in ((1, up), (2, opp), (3, down)):
        send(r.picky.at[y], r.picky.at[y], "py", step, (peer, g))

    for i in range(4):
        rows = slice(i * 256, (i + 1) * 256)
        r.tgrad[rows, :] = dot_nt(r.fb[rows, :HID], r.sf[...]) + dot_nt(r.fb[rows, HID:], r.nf[...])

    for step in (1, 2, 3):
        arrived(r.picky.at[lax.rem(y + 4 - step, 4)], "py", step)
    mixed = r.picky[0].astype(F32) + r.picky[1].astype(F32)
    mixed = mixed + r.picky[2].astype(F32) + r.picky[3].astype(F32)
    r.pickall[c] = mixed.astype(BF16)
    send(r.pickall.at[c], r.pickall.at[c], "ps", 0, (sib, g))

    arrived(r.wgin, "a1", 0)
    r.wg1[...] = (r.wg[c].astype(F32) + r.wgin[...].astype(F32)).astype(BF16)
    r.wgy[y] = r.wg1[y]
    for step, peer_y in ((1, lax.rem(y + 1, 4)), (2, lax.rem(y + 2, 4)), (3, lax.rem(y + 3, 4))):
        send(r.wg1.at[peer_y], r.wgy.at[y], "a2", step, (peer_y * 2 + c, g))

    arrived(r.pickall.at[1 - c], "ps", 0)
    rows32 = r.pickall[...].reshape(32, 2 * HID)
    node_grad = dot_nt(rows32[:, :HID], r.sf[...]) + dot_nt(rows32[:, HID:], r.nf[...])
    r.nodeg[...] = node_grad
    for i in range(4):
        r.ngrad[i : i + 1, :] = r.nodeg[pl.ds(t * 4 + i, 1), :]
    small = (node_grad * (1.0 / SEQ)).astype(BF16)
    r.act[...] = dot_nt(small, r.wo[...])

    def pre_grad(n, carry):
        slot = n // 4
        rows = pl.ds(pl.multiple_of((n % 4) * SEQ, SEQ), SEQ)
        r.pre[slot, rows, :] = (r.act[pl.ds(n, 1), :] * r.slope[slot, rows, :]).astype(BF16)
        return carry

    lax.fori_loop(0, 32, pre_grad, 0)
    pre_all = r.pre[...].reshape(NT * 256, CHUNK)
    norm_all = r.normed[...].reshape(NT * 256, D)
    for i in range(3):
        cols = slice(i * 128, (i + 1) * 128)
        r.gfull[0, cols, :] = dot_tn(pre_all[:, cols], norm_all) * TEXT_SCALE
    a_high, a_low = split(r.asum[...])
    r.gfull[1] = (dot_tn(a_high, small) + dot_tn(a_low, small)) * TEXT_SCALE

    def pack(k, carry):
        rows = pl.ds(pl.multiple_of(k * OWN, 8), OWN)
        both = jnp.concatenate([r.gfull[0, rows, :], r.gfull[1, rows, :]], axis=0)
        r.gpack[k] = both.astype(BF16)
        return carry

    lax.fori_loop(0, NG, pack, 0)
    r.grecv[g] = r.gpack[g]
    scatter(lambda to: r.gpack.at[to], r.grecv, "gr")

    for step in (1, 2, 3):
        arrived(r.wgy.at[lax.rem(y + 4 - step, 4)], "a2", step)
    quarter = r.wgy[0].astype(F32) + r.wgy[1].astype(F32)
    quarter = quarter + r.wgy[2].astype(F32) + r.wgy[3].astype(F32)
    r.wg2[...] = quarter.astype(BF16)
    r.wgg[g] = r.wg2[g]
    scatter(lambda to: r.wg2.at[to], r.wgg, "a3")

    arrived(r.hid.at[RIM + ROWS :], "rim", 4)
    arrived(r.hid.at[:RIM], "rim", 5)
    for i in range(6):
        rows = slice(i * 256, (i + 1) * 256)
        r.proj2[rows, :] = dot(r.hid[rows, :], r.ns[...]).astype(BF16)
    for i in range(4):
        rows = slice(i * 256, (i + 1) * 256)
        ext = slice(RIM + i * 256, RIM + (i + 1) * 256)
        r.gnn[rows, :] = (dot(r.hid[ext, :], r.ss[...]) + dot(r.e[rows, :], r.proj2[...])).astype(BF16)

    scatter_wait(r.wgg, "a3")
    piece = r.wgg[0].astype(F32)
    for k in range(1, NG):
        piece = piece + r.wgg[k].astype(F32)
    r.wgall[c, y, g] = piece.astype(BF16)
    own_piece = r.wgall.at[c, y, g]

    def piece_out(k, to, source):
        send(own_piece, own_piece, "a4", k, (t, to), start=False).start()

    each_peer(piece_out)

    scatter_wait(r.grecv, "gr")
    summed = r.grecv[0].astype(F32)
    for k in range(1, NG):
        summed = summed + r.grecv[k].astype(F32)
    r.gin[...] = summed[:OWN]
    r.gout[...] = summed[OWN:]

    each_peer(lambda k, to, source: arrived(r.wgall.at[c, y, source], "a4", k))
    own_quarter = r.wgall.at[c, y]
    for step, peer in ((1, up), (2, opp), (3, down)):
        send(own_quarter, own_quarter, "a5", step, (peer, g))
    for step in (1, 2, 3):
        arrived(r.wgall.at[c, lax.rem(y + 4 - step, 4)], "a5", step)
    own_side = r.wgall.at[c]
    send(own_side, own_side, "a6", 0, (sib, g))
    arrived(r.wgall.at[1 - c], "a6", 0)
    for side, first, second in ((0, r.gsf, r.gss), (1, r.gnf, r.gns)):
        for q in range(3):
            first[q * 256 : (q + 1) * 256, :] = r.wgall[side, q].astype(F32).reshape(256, HID)
        second[...] = r.wgall[side, 3].astype(F32).reshape(256, HID)

    for copy in pending:
        copy.wait_send()
    scatter_sent(r.wpack.at[g], "w")
    scatter_sent(own_emb, "eg")
    each_peer(lambda k, to, source: send(own_emb, own_emb, "es", k, (sib, g), start=False).wait_send())
    scatter_sent(r.pick1.at[0], "pg")
    scatter_sent(r.gpack.at[0], "gr")
    scatter_sent(r.wg2.at[0], "a3")
    scatter_sent(own_piece, "a4")


def per_device(states, w_in, w_out, table, adj, sources, node_ids, sf, nf, ss, ns, ups):
    vmem = pl.BlockSpec(memory_space=pltpu.VMEM)
    specs = [vmem] * len(INPUTS)
    specs[INPUTS.index("src")] = pl.BlockSpec(memory_space=pltpu.SMEM)
    scratch = [pltpu.VMEM(shape, dtype) for shape, dtype in SCRATCH.values()]
    for count in SEMS.values():
        scratch += [pltpu.SemaphoreType.DMA((count,)), pltpu.SemaphoreType.DMA((count,))]
    return pl.pallas_call(
        body,
        out_shape=tuple(jax.ShapeDtypeStruct(*spec) for spec in OUTPUTS.values()),
        in_specs=specs,
        out_specs=tuple([vmem] * len(OUTPUTS)),
        scratch_shapes=scratch,
        compiler_params=pltpu.CompilerParams(
            collective_id=0, has_side_effects=True, vmem_limit_bytes=62 * 1024 * 1024
        ),
    )(
        states.reshape(4 * SEQ, D), w_in, w_out, table, adj.reshape(32, 128, 128),
        sources, node_ids.reshape(1, NFT), sf, nf, ss, ns, ups,
    )


def solution(mesh):
    both = ("text", "graph")
    rows = P(both, None)
    return jax.shard_map(
        per_device,
        mesh=mesh,
        in_specs=(
            P(both, None, None), rows, rows, rows, P(both, None, None, None), rows,
            P(), P(), P(), P(), P(), rows,
        ),
        out_specs=(rows, rows, rows, rows, rows, P(), P(), P(), P()),
        check_vma=False,
    )
```

time: 767 us -> 134 us (0.17); the launches traced: 757 us -> 134 us
  waiting for transfers between devices: 492 us -> 0 us
  Pallas kernels: 0 us -> 121 us
  blocking collectives: 68 us -> 0 us
  local copies, waits for them, and re-layouts: 76.1 us -> 12.2 us
  matrix products: 58.5 us -> 0 us
  other arithmetic: 27.2 us -> 0 us
  starting transfers between devices: 21.1 us -> 0 us
  between operations: 14.5 us -> 0.67 us
    unnamed x6 -> x0, waiting for transfers between devices: 374 us -> none
    pallas_call x0 -> x1, Pallas kernels: none -> 121 us  [per_device(): pl.pallas_call(body, out_shape=tuple((jax.ShapeDtypeStruct(*spec) for spe...]
    all_gather x2 -> x0, waiting for transfers between devices: 110 us -> none  [the longest x1 62.2 us: per_device(): out_full = lax.all_gather(weight_out, ('text', 'graph'), axis=0, tiled=True)]
    all_gather x1 -> x0, blocking collectives: 68 us -> none  [per_device(): lax.all_gather(embedded, ('text', 'graph'), axis=0, tiled=True)]
    dot_general x22 -> x0, matrix products: 58.5 us -> none  [the longest x6 21.5 us: inner_rows(): lax.dot_general(left, right, (((0,), (0,)), ((), ())), preferred_element_...]
    unnamed x71 -> x24, local copies, waits for them, and re-layouts: 35.4 us -> 12.2 us
    ppermute x8 -> x0, starting transfers between devices: 21 us -> none  [the longest x4 11.2 us: passed_along(): lax.ppermute(array, axis, [(i, (i + by) % size) for i in range(size)])]
    slice x13 -> x0, local copies, waits for them, and re-layouts: 19.8 us -> none  [the longest x4 8.52 us: return_rims(): own_rows = extended[rim_rows:rim_rows + row_count]]
  transfers between devices with their start and end apart: 12 -> 0, of which waited for: 6 -> 0; matrix products, arithmetic and copies ran while one was open for 8% -> 0% of each run, Pallas kernels for 0% -> 0%
where the time goes in v1:
time: 134 us
  Pallas kernels  121 us (90%)
  local copies, waits for them, and re-layouts  12.2 us (9%)
    pallas_call x1, Pallas kernels, per_device(): pl.pallas_call(body, out_shape=tuple((jax.ShapeDtypeStruct(*spec) for spe...  121 us
    unnamed x24, local copies, waits for them, and re-layouts  12.2 us

profile of v1, /device:TPU:1, one launch (start us, length us, event | category | flops | bytes accessed | tf_op | source)
XLA Modules:
  0.0 133.5 jit_solution(3006537822778843163)
XLA Ops:
  0.6 1.3 %copy.21.refs_5_ = s32[8,4]{1,0:T(8,128)} copy(s32[8,4]{0,1:T(4,128)} %param.17) | data formatting | bytes 256 | tf_op args[5]
  2.0 120.7 %shard_map.187 = (bf16[1024,256]{1,0:T(8,128)(2,1)}, f32[1024,768]{1,0:T(8,128)}, f32[4,768]{1,0:T(4,128)}, f32[24,768]{1,0:T(8,128)}, f32[24,768]{1,0:T(8,128)}...) custom-call(bf16[256,768]{1,0:T(8,128)(2,1)} %bitcast.4, ...), custom_call_target="tpu_custom_call" | custom-call | tf_op jit(solution)/shard_map/pallas_call | solution.py:569
  122.7 1.9 %copy.31 = bf16[1024,256]{1,0:T(8,128)(2,1)} copy(bf16[1024,256]{1,0:T(8,128)(2,1)} %get-tuple-element.18) | data formatting | bytes 1048576
  124.6 0.0 copy-start.6
  124.6 0.0 copy-start.5
  124.6 0.0 copy-start.4
  124.6 0.0 copy-start.1
  124.6 0.0 copy-start
  124.6 3.9 %copy.32 = f32[1024,768]{1,0:T(8,128)} copy(f32[1024,768]{1,0:T(8,128)} %get-tuple-element.19) | data formatting | bytes 6291456
  128.5 0.0 copy-done.6
  128.5 0.0 copy-start.3
  128.5 0.0 copy-start.2
  128.5 0.6 copy.33
  129.1 0.0 copy-done.5
  129.1 0.6 copy.34
  129.7 0.0 copy-done.4
  129.7 0.6 copy.35
  130.4 0.0 copy-done.1
  130.4 0.9 copy.36
  131.2 0.0 copy-done
  131.2 0.9 copy.37
  132.1 0.0 copy-done.3
  132.1 0.7 copy.38
  132.8 0.0 copy-done.2
  132.8 0.7 copy.39
Async XLA Ops:
  124.6 3.9 %copy-start.6 = (f32[4,768]{1,0:T(4,128)S(1)}, f32[4,768]{1,0:T(4,128)}, u32[]{:S(2)}) copy-start(f32[4,768]{1,0:T(4,128)} %get-tuple-element.20) | copy-start | bytes 36868
  124.6 4.5 %copy-start.5 = (f32[24,768]{1,0:T(8,128)S(1)}, f32[24,768]{1,0:T(8,128)}, u32[]{:S(2)}) copy-start(f32[24,768]{1,0:T(8,128)} %get-tuple-element.21) | copy-start | bytes 221188
  124.6 5.1 %copy-start.4 = (f32[24,768]{1,0:T(8,128)S(1)}, f32[24,768]{1,0:T(8,128)}, u32[]{:S(2)}) copy-start(f32[24,768]{1,0:T(8,128)} %get-tuple-element.22) | copy-start | bytes 221188
  124.6 5.8 %copy-start.1 = (f32[768,256]{1,0:T(8,128)S(1)}, f32[768,256]{1,0:T(8,128)}, u32[]{:S(2)}) copy-start(f32[768,256]{1,0:T(8,128)} %get-tuple-element.23) | copy-start | bytes 2359300
  124.6 6.7 %copy-start = (f32[768,256]{1,0:T(8,128)S(1)}, f32[768,256]{1,0:T(8,128)}, u32[]{:S(2)}) copy-start(f32[768,256]{1,0:T(8,128)} %get-tuple-element.24) | copy-start | bytes 2359300
  128.5 3.6 %copy-start.3 = (f32[256,256]{1,0:T(8,128)S(1)}, f32[256,256]{1,0:T(8,128)}, u32[]{:S(2)}) copy-start(f32[256,256]{1,0:T(8,128)} %get-tuple-element.25) | copy-start | bytes 786436
  128.5 4.3 %copy-start.2 = (f32[256,256]{1,0:T(8,128)S(1)}, f32[256,256]{1,0:T(8,128)}, u32[]{:S(2)}) copy-start(f32[256,256]{1,0:T(8,128)} %get-tuple-element.26) | copy-start | bytes 786436

commit v2 on v1

--- a/solution.py
+++ b/solution.py
@@ -27,25 +27,33 @@
 NODE_SCALE = 1.0 / math.sqrt(131072)
 TEXT_SCALE = 1.0 / math.sqrt(NFT)
 
-INPUTS = (
-    "states", "w_in", "w_out", "table", "adj", "src", "ids",
-    "sf", "nf", "ss", "ns", "ups",
-)
-OUTPUTS = {
+INPUTS = {
+    "states": ((4 * SEQ, D), BF16),
+    "w_in": ((OWN, D), BF16),
+    "w_out": ((OWN, D), BF16),
+    "ids": ((1, NFT), jnp.int32),
+    "src": ((4, 8), jnp.int32),
+    "adj": ((32, 128, 128), BF16),
+    "ups": ((ROWS, HID), BF16),
+    "table": ((ROWS, D), BF16),
+    "sf": ((D, HID), BF16),
+    "nf": ((D, HID), BF16),
+    "ss": ((HID, HID), BF16),
+    "ns": ((HID, HID), BF16),
+}
+HANDED = {
     "gnn": ((ROWS, HID), BF16),
-    "tgrad": ((ROWS, D), F32),
+    "fb": ((ROWS, 2 * HID), BF16),
+    "early": ((2, 4, 20, 16, 128), BF16),
+    "late": ((2, 48, 16, 128), BF16),
     "ngrad": ((4, D), F32),
     "gin": ((OWN, D), F32),
     "gout": ((OWN, D), F32),
-    "gsf": ((D, HID), F32),
-    "gnf": ((D, HID), F32),
-    "gss": ((HID, HID), F32),
-    "gns": ((HID, HID), F32),
 }
 SCRATCH = {
-    "wpack": ((NG, 2 * OWN, D), BF16),
-    "wide_in": ((CHUNK, D), F32),
-    "wide_out": ((CHUNK, D), F32),
+    "pack_in": ((NG, 2 * OWN, D // 2), BF16),
+    "pack_out": ((NG, 2 * OWN, D // 2), BF16),
+    "wide": ((CHUNK, D), F32),
     "wi": ((CHUNK, D), BF16),
     "wo": ((CHUNK, D), BF16),
     "normed": ((NT, 256, D), BF16),
@@ -53,6 +61,9 @@
     "before": ((256, CHUNK), F32),
     "slope": ((NT, 256, CHUNK), F32),
     "asum": ((32, CHUNK), F32),
+    "spread": ((128, CHUNK), F32),
+    "turned": ((CHUNK, 128), F32),
+    "acols": ((NG, OWN, 128), F32),
     "part": ((32, D), F32),
     "part2": ((2, 16, D), F32),
     "pairin": ((16, D), F32),
@@ -74,35 +85,39 @@
     "embproj": ((NFT, 2 * HID), BF16),
     "hid": ((EXT, HID), BF16),
     "proj2": ((EXT, HID), BF16),
-    "fb": ((ROWS, 2 * HID), BF16),
     "b1": ((EXT, HID), F32),
     "b1b": ((EXT, HID), BF16),
     "b1in": ((2, RIM, HID), BF16),
     "feat": ((ROWS, D), BF16),
-    "wg": ((2, 4, NG, 16, HID), BF16),
-    "wgin": ((4, NG, 16, HID), BF16),
-    "wg1": ((4, NG, 16, HID), BF16),
-    "wgy": ((4, NG, 16, HID), BF16),
-    "wg2": ((NG, 16, HID), BF16),
-    "wgg": ((NG, 16, HID), BF16),
-    "wgall": ((2, 4, NG, 16, HID), BF16),
+    "e0": ((2, 80, 16, 128), BF16),
+    "e1in": ((80, 16, 128), BF16),
+    "e1": ((80, 16, 128), BF16),
+    "e2": ((4, 20, 16, 128), BF16),
+    "e3out": ((20, 16, 128), BF16),
+    "e3": ((NG, 2, 16, 128), BF16),
+    "l0": ((2, 48, 16, 128), BF16),
+    "l1in": ((48, 16, 128), BF16),
+    "l1": ((48, 16, 128), BF16),
+    "l2": ((NG, 3, 16, 128), BF16),
+    "l3": ((4, 3, 16, 128), BF16),
     "pick": ((2, NG, 16, 2 * HID), BF16),
     "pickin": ((NG, 16, 2 * HID), BF16),
     "pick1": ((NG, 16, 2 * HID), BF16),
     "pickg": ((NG, 16, 2 * HID), BF16),
     "picky": ((4, 16, 2 * HID), BF16),
-    "pickall": ((2, 16, 2 * HID), BF16),
+    "pickall": ((NG, 2, 16, 2 * HID), BF16),
     "nodeg": ((32, D), F32),
     "act": ((32, CHUNK), F32),
     "pre": ((NT, 256, CHUNK), BF16),
-    "gfull": ((2, CHUNK, D), F32),
-    "gpack": ((NG, 2 * OWN, D), BF16),
-    "grecv": ((NG, 2 * OWN, D), BF16),
+    "gfull": ((CHUNK, D), F32),
+    "gpack": ((NG, 2 * OWN, D // 2), BF16),
+    "grecv": ((NG, 2 * OWN, D // 2), BF16),
 }
 SEMS = {
-    "w": 16, "st": 9, "rim": 8, "pair": 1, "ye": 4, "eg": 16, "es": 16,
-    "pk": 1, "pg": 16, "py": 4, "ps": 1,
-    "a1": 1, "a2": 4, "a3": 16, "a4": 16, "a5": 4, "a6": 1, "gr": 16,
+    "wi": 16, "wo": 16, "st": 9, "rim": 8, "pair": 1, "ye": 4, "eg": 16, "es": 16,
+    "ac": 16, "pk": 1, "pg": 16, "py": 4, "ps": 1, "ag": 16, "as": 16,
+    "e1": 1, "e2": 4, "e3": 16, "e4": 16, "e5": 4, "e6": 1,
+    "l1": 1, "l2": 16, "l3": 4, "l4": 16, "l5": 1, "gr": 16,
 }
 
 
@@ -129,13 +144,31 @@
 
 
 def body(*refs):
-    names = list(INPUTS) + list(OUTPUTS) + list(SCRATCH)
-    r = SimpleNamespace(**dict(zip(names, refs)))
-    sems = {}
-    at = len(names)
-    for name in SEMS:
-        sems[name] = (refs[at], refs[at + 1])
-        at += 2
+    taken = iter(refs)
+    given = {name: next(taken) for name in INPUTS}
+    handed = {name: next(taken) for name in HANDED}
+    r = SimpleNamespace()
+    for name in (*INPUTS, *HANDED, *SCRATCH):
+        setattr(r, name, next(taken))
+    sems = {name: (next(taken), next(taken)) for name in SEMS}
+    fetch_sems, hand_sems = next(taken), next(taken)
+    fetches = {
+        name: pltpu.make_async_copy(given[name], getattr(r, name), fetch_sems.at[k])
+        for k, name in enumerate(INPUTS)
+    }
+    for copy in fetches.values():
+        copy.start()
+    handing = []
+
+    def fetched(*wanted):
+        for name in wanted:
+            fetches[name].wait()
+
+    def hand(name):
+        at = list(HANDED).index(name)
+        copy = pltpu.make_async_copy(getattr(r, name), handed[name], hand_sems.at[at])
+        copy.start()
+        handing.append(copy)
 
     t = lax.axis_index("text")
     g = lax.axis_index("graph")
@@ -147,6 +180,14 @@
         return lax.rem(y + step, 4) * 2 + c
 
     up, opp, down = at_y(1), at_y(2), at_y(3)
+    x, z = lax.div(g, 4), lax.rem(g, 4)
+
+    def at_x(step):
+        return lax.rem(x + step, 4)
+
+    def at_z(step):
+        return lax.rem(z + step, 4)
+
     ahead = lax.rem(g + 1, NG)
     behind = lax.rem(g + NG - 1, NG)
     pending = []
@@ -197,59 +238,80 @@
     for peer in (sib, up, opp, down):
         greet((peer, g))
     each_peer(lambda k, to, source: greet((t, to)))
-    pl.semaphore_wait(barrier, 19)
-
-    both = jnp.concatenate([r.w_in[...].astype(F32), r.w_out[...].astype(F32)], axis=0)
-    r.wpack[g] = both.astype(BF16)
-    scatter(lambda to: r.wpack.at[g], r.wpack, "w")
+
+    fetched("w_in", "w_out", "states")
+
+    def halves(rows):
+        return jnp.concatenate([rows[:, : D // 2], rows[:, D // 2 :]], axis=0)
+
+    def joined(rows):
+        return jnp.concatenate([rows[:OWN], rows[OWN:]], axis=1)
+
+    r.pack_in[g] = halves(r.w_in[...].astype(F32)).astype(BF16)
+    r.pack_out[z * 4 + x] = halves(r.w_out[...].astype(F32)).astype(BF16)
 
     for i in range(4):
-        x = r.states[i * SEQ : (i + 1) * SEQ, :].astype(F32)
-        r.smean[i : i + 1, :] = jnp.sum(x, axis=0, keepdims=True) * (1.0 / SEQ)
-        mean = jnp.mean(x, axis=1, keepdims=True)
-        centered = x - mean
+        own = r.states[i * SEQ : (i + 1) * SEQ, :].astype(F32)
+        r.smean[i : i + 1, :] = jnp.sum(own, axis=0, keepdims=True) * (1.0 / SEQ)
+        mean = jnp.mean(own, axis=1, keepdims=True)
+        centered = own - mean
         var = jnp.mean(centered * centered, axis=1, keepdims=True)
         r.normed[t, i * SEQ : (i + 1) * SEQ, :] = (centered * lax.rsqrt(var + 1e-05)).astype(BF16)
+    fetched("table", "sf", "nf")
+    for i in range(4):
+        rows = slice(i * 256, (i + 1) * 256)
+        nodes = r.table[rows, :]
+        r.tn[RIM + i * 256 : RIM + (i + 1) * 256, :] = dot(nodes, r.nf[...]).astype(BF16)
+        r.tself[rows, :] = dot(nodes, r.sf[...])
+
+    pl.semaphore_wait(barrier, 19)
+    own_in, own_out = r.pack_in.at[g], r.pack_out.at[z * 4 + x]
+    for step in (1, 3, 2):
+        send(own_in, own_in, "wi", step, (t, x * 4 + at_z(step)))
+        send(own_out, own_out, "wo", step, (t, at_x(step) * 4 + z))
     mine = r.normed.at[t]
     send(mine, mine, "st", 0, (sib, g))
     send(mine, mine, "st", 1, (up, g))
     send(mine, mine, "st", 2, (down, g))
 
-    for i in (0, 3, 1, 2):
-        rows = slice(i * 256, (i + 1) * 256)
-        x = r.table[rows, :]
-        r.tn[RIM + i * 256 : RIM + (i + 1) * 256, :] = dot(x, r.nf[...]).astype(BF16)
-        r.tself[rows, :] = dot(x, r.sf[...])
-        if i == 3:
-            send(r.tn.at[RIM : 2 * RIM], r.tn.at[RIM + ROWS :], "rim", 0, (t, behind))
-            send(r.tn.at[ROWS : ROWS + RIM], r.tn.at[:RIM], "rim", 1, (t, ahead))
-
+    fetched("adj", "src")
     def tiles(b, carry):
         rows = pl.ds(pl.multiple_of(b * 128, 128), 128)
         plain = [r.adj[b * 4 + k] for k in range(4)]
         turned = [p.astype(F32).T.astype(BF16) for p in plain]
+        here = lax.broadcasted_iota(jnp.int32, (4, 8), 1) == b
+        source = jnp.sum(jnp.where(here, r.src[...].astype(F32), 0.0), axis=1, keepdims=True)
         for s in range(12):
+            hits = jnp.where(source == float(s), 1.0, 0.0)
             own = jnp.zeros((128, 128), BF16)
             other = jnp.zeros((128, 128), BF16)
             for k in range(4):
-                hit = r.src[b, k] == s
-                own = own + jnp.where(hit, plain[k], jnp.zeros_like(plain[k]))
-                other = other + jnp.where(hit, turned[k], jnp.zeros_like(turned[k]))
+                hit = jnp.broadcast_to(hits[k : k + 1, :], (128, 128)).astype(BF16)
+                own = own + plain[k] * hit
+                other = other + turned[k] * hit
             r.e[rows, s * 128 : (s + 1) * 128] = own
             r.et[s * 128 : (s + 1) * 128, rows] = other
         return carry
 
     lax.fori_loop(0, 8, tiles, 0)
 
+    for step in (1, 2, 3):
+        arrived(r.pack_in.at[x * 4 + at_z(4 - step)], "wi", step)
+    slab = r.pack_in.at[pl.ds(x * 4, 4)]
+    for step in (1, 3, 2):
+        send(slab, slab, "wi", 4 + step, (t, at_x(step) * 4 + z))
+    for step in (1, 2, 3):
+        arrived(r.pack_out.at[z * 4 + at_x(4 - step)], "wo", step)
+    slab = r.pack_out.at[pl.ds(z * 4, 4)]
+    for step in (1, 3, 2):
+        send(slab, slab, "wo", 4 + step, (t, x * 4 + at_z(step)))
+
+    fetched("ups", "ss", "ns")
     for i in (0, 5, 1, 2, 3, 4):
         rows = slice(i * 256, (i + 1) * 256)
         r.b2[rows, :] = dot(r.et[rows, :], r.ups[...])
-        if i == 5:
-            r.b2out[0] = r.b2[:RIM, :].astype(BF16)
-            r.b2out[1] = r.b2[RIM + ROWS :, :].astype(BF16)
-            send(r.b2out.at[0], r.b2in.at[1], "rim", 2, (t, behind))
-            send(r.b2out.at[1], r.b2in.at[0], "rim", 3, (t, ahead))
-
+
+    fetched("ids")
     row = lax.broadcasted_iota(jnp.int32, (NFT, NFT), 0)
     col = lax.broadcasted_iota(jnp.int32, (NFT, NFT), 1)
     wanted = (col & 256) + ((col >> 2) & 3) * 64 + ((col >> 4) & 15) * 4 + (col & 3)
@@ -273,18 +335,18 @@
         across = lax.broadcasted_iota(jnp.int32, (NFT, 128), 1).astype(F32) + start
         r.oht[:, e * 128 : (e + 1) * 128] = jnp.where(across == spot_col, 1.0, 0.0).astype(BF16)
 
-    scatter_wait(r.wpack, "w")
-
-    def unpack(k, carry):
-        block = r.wpack[k].astype(F32)
-        rows = pl.ds(pl.multiple_of(k * OWN, 8), OWN)
-        r.wide_in[rows, :] = block[:OWN]
-        r.wide_out[rows, :] = block[OWN:]
-        return carry
-
-    lax.fori_loop(0, NG, unpack, 0)
-    r.wi[...] = r.wide_in[...].astype(BF16)
-    r.wo[...] = r.wide_out[...].astype(BF16)
+    def unpack(packed, out, place):
+        def step(k, carry):
+            rows = pl.ds(pl.multiple_of(k * OWN, 8), OWN)
+            r.wide[rows, :] = joined(packed[place(k)].astype(F32))
+            return carry
+
+        lax.fori_loop(0, NG, step, 0)
+        out[...] = r.wide[...].astype(BF16)
+
+    for step in (1, 2, 3):
+        arrived(r.pack_in.at[pl.ds(at_x(4 - step) * 4, 4)], "wi", 4 + step)
+    unpack(r.pack_in, r.wi, lambda k: k)
 
     def encode(slot):
         r.before[...] = dot_nt(r.normed[slot], r.wi[...])
@@ -311,6 +373,12 @@
     send(from_up, from_up, "st", 6, (sib, g))
     arrived(r.normed.at[sib], "st", 0)
     encode(sib)
+    send(r.tn.at[RIM : 2 * RIM], r.tn.at[RIM + ROWS :], "rim", 0, (t, behind))
+    send(r.tn.at[ROWS : ROWS + RIM], r.tn.at[:RIM], "rim", 1, (t, ahead))
+    r.b2out[0] = r.b2[:RIM, :].astype(BF16)
+    r.b2out[1] = r.b2[RIM + ROWS :, :].astype(BF16)
+    send(r.b2out.at[0], r.b2in.at[1], "rim", 2, (t, behind))
+    send(r.b2out.at[1], r.b2in.at[0], "rim", 3, (t, ahead))
     encode(down)
     encode(up)
     arrived(far.at[:128], "st", 3)
@@ -327,6 +395,9 @@
     arrived(far_pair.at[128:], "st", 8)
     encode(fellow(opp))
 
+    for step in (1, 2, 3):
+        arrived(r.pack_out.at[pl.ds(at_z(4 - step) * 4, 4)], "wo", 4 + step)
+    unpack(r.pack_out, r.wo, lambda k: (k % 4) * 4 + k // 4)
     a_high, a_low = split(r.asum[...] * (1.0 / SEQ))
     r.part[...] = dot(a_high, r.wo[...]) + dot(a_low, r.wo[...])
     for i in range(4):
@@ -353,6 +424,12 @@
     own_emb = r.emb.at[c, g]
     send(own_emb, own_emb, "es", 0, (sib, g))
 
+    r.spread[...] = jnp.zeros_like(r.spread)
+    r.spread[pl.ds(pl.multiple_of(lax.rem(g, 4) * 32, 32), 32), :] = r.asum[...]
+    r.turned[...] = r.spread[...].T
+    my_units = pl.ds(pl.multiple_of(g * OWN, 8), OWN)
+    r.acols[g] = r.turned[my_units, :]
+
     arrived(r.b2in.at[0], "rim", 3)
     arrived(r.b2in.at[1], "rim", 2)
     r.b2[RIM : 2 * RIM, :] = r.b2[RIM : 2 * RIM, :] + r.b2in[0].astype(F32)
@@ -373,6 +450,8 @@
     arrived(r.emb.at[1 - c, g], "es", 0)
     each_peer(lambda k, to, source: arrived(r.emb.at[1 - c, source], "es", k))
 
+    scatter(lambda to: r.turned.at[pl.ds(pl.multiple_of(to * OWN, 8), OWN)], r.acols, "ac")
+
     emb_all = r.emb[...].reshape(NFT, D)
     r.embproj[:, :HID] = dot(emb_all, r.sf[...]).astype(BF16)
     r.embproj[:, HID:] = dot(emb_all, r.nf[...]).astype(BF16)
@@ -389,8 +468,6 @@
         value, slope = gelu_pair(pre)
         r.hid[ext, :] = value.astype(BF16)
         r.fb[rows, :HID] = (r.hg[rows, :] * slope).astype(BF16)
-    send(r.hid.at[RIM : 2 * RIM], r.hid.at[RIM + ROWS :], "rim", 4, (t, behind))
-    send(r.hid.at[ROWS : ROWS + RIM], r.hid.at[:RIM], "rim", 5, (t, ahead))
     for i in (0, 5, 1, 2, 3, 4):
         rows = slice(i * 256, (i + 1) * 256)
         term = dot(r.et[rows, :], r.fb[:, :HID])
@@ -413,62 +490,83 @@
         old = r.table[rows, :].astype(F32) * r.keep[ext, :]
         r.feat[rows, :] = (old + dot(r.oh[ext, :], emb_all)).astype(BF16)
 
-    features(0)
-    features(1)
+    for i in range(4):
+        features(i)
     arrived(r.pickin, "pk", 0)
     r.pick1[...] = (r.pick[c].astype(F32) + r.pickin[...].astype(F32)).astype(BF16)
     r.pickg[g] = r.pick1[g]
     scatter(lambda to: r.pick1.at[to], r.pickg, "pg")
-    features(2)
-    features(3)
+
+    def keep_grad(buffer, first, left, right):
+        for q in range(left.shape[1] // 256):
+            term = dot_tn(left[:, q * 256 : (q + 1) * 256], right) * NODE_SCALE
+            at = slice(first + q * 16, first + q * 16 + 16)
+            for side in range(2):
+                cols = slice(side * 128, (side + 1) * 128)
+                buffer[side, at] = term[:, cols].astype(BF16).reshape(16, 16, 128)
+
+    hidden = r.hid[RIM : RIM + ROWS, :]
+    keep_grad(r.e0, 48, hidden, r.ups[...])
+    keep_grad(r.e0, 64, hidden, r.back2[...])
+    keep_grad(r.e0, 0, r.feat, r.fb[:, :HID])
+    send(r.e0.at[1 - c], r.e1in, "e1", 0, (sib, g))
 
     arrived(r.b1in.at[0], "rim", 7)
     arrived(r.b1in.at[1], "rim", 6)
     r.b1[RIM : 2 * RIM, :] = r.b1[RIM : 2 * RIM, :] + r.b1in[0].astype(F32)
     r.b1[ROWS : ROWS + RIM, :] = r.b1[ROWS : ROWS + RIM, :] + r.b1in[1].astype(F32)
     r.fb[:, HID:] = r.b1[RIM : RIM + ROWS, :].astype(BF16)
-
-    for side in range(2):
-        cols = slice(side * HID, (side + 1) * HID)
-        for q in range(3):
-            term = dot_tn(r.feat[:, q * 256 : (q + 1) * 256], r.fb[:, cols])
-            r.wg[side, q] = (term * NODE_SCALE).astype(BF16).reshape(NG, 16, HID)
-    hidden = r.hid[RIM : RIM + ROWS, :]
-    r.wg[0, 3] = (dot_tn(hidden, r.ups[...]) * NODE_SCALE).astype(BF16).reshape(NG, 16, HID)
-    r.wg[1, 3] = (dot_tn(hidden, r.back2[...]) * NODE_SCALE).astype(BF16).reshape(NG, 16, HID)
-    send(r.wg.at[1 - c], r.wgin, "a1", 0, (sib, g))
+    hand("fb")
+    arrived(r.e1in, "e1", 0)
+    r.e1[...] = (r.e0[c].astype(F32) + r.e1in[...].astype(F32)).astype(BF16)
+    r.e2[y] = r.e1[pl.ds(y * 20, 20)]
+    for step in (1, 3, 2):
+        to_y = lax.rem(y + step, 4)
+        send(r.e1.at[pl.ds(to_y * 20, 20)], r.e2.at[y], "e2", step, (to_y * 2 + c, g))
+    keep_grad(r.l0, 0, r.feat, r.fb[:, HID:])
+    send(r.l0.at[1 - c], r.l1in, "l1", 0, (sib, g))
+
+    def over_peers(ref):
+        total = ref[0].astype(F32)
+        for k in range(1, NG):
+            total = total + ref[k].astype(F32)
+        return total
+
+    def over_y(ref):
+        return (ref[0].astype(F32) + ref[1].astype(F32)) + (ref[2].astype(F32) + ref[3].astype(F32))
 
     scatter_wait(r.pickg, "pg")
-    mixed = r.pickg[0].astype(F32)
-    for k in range(1, NG):
-        mixed = mixed + r.pickg[k].astype(F32)
-    r.picky[y] = mixed.astype(BF16)
+    r.picky[y] = over_peers(r.pickg).astype(BF16)
     for step, peer in ((1, up), (2, opp), (3, down)):
         send(r.picky.at[y], r.picky.at[y], "py", step, (peer, g))
-
-    for i in range(4):
-        rows = slice(i * 256, (i + 1) * 256)
-        r.tgrad[rows, :] = dot_nt(r.fb[rows, :HID], r.sf[...]) + dot_nt(r.fb[rows, HID:], r.nf[...])
-
+    arrived(r.l1in, "l1", 0)
+    r.l1[...] = (r.l0[c].astype(F32) + r.l1in[...].astype(F32)).astype(BF16)
+    r.l2[g] = r.l1[pl.ds(g * 3, 3)]
+    scatter(lambda to: r.l1.at[pl.ds(to * 3, 3)], r.l2, "l2")
     for step in (1, 2, 3):
         arrived(r.picky.at[lax.rem(y + 4 - step, 4)], "py", step)
-    mixed = r.picky[0].astype(F32) + r.picky[1].astype(F32)
-    mixed = mixed + r.picky[2].astype(F32) + r.picky[3].astype(F32)
-    r.pickall[c] = mixed.astype(BF16)
-    send(r.pickall.at[c], r.pickall.at[c], "ps", 0, (sib, g))
-
-    arrived(r.wgin, "a1", 0)
-    r.wg1[...] = (r.wg[c].astype(F32) + r.wgin[...].astype(F32)).astype(BF16)
-    r.wgy[y] = r.wg1[y]
-    for step, peer_y in ((1, lax.rem(y + 1, 4)), (2, lax.rem(y + 2, 4)), (3, lax.rem(y + 3, 4))):
-        send(r.wg1.at[peer_y], r.wgy.at[y], "a2", step, (peer_y * 2 + c, g))
-
-    arrived(r.pickall.at[1 - c], "ps", 0)
-    rows32 = r.pickall[...].reshape(32, 2 * HID)
-    node_grad = dot_nt(rows32[:, :HID], r.sf[...]) + dot_nt(rows32[:, HID:], r.nf[...])
+    r.pickall[g, c] = over_y(r.picky).astype(BF16)
+    own_picks = r.pickall.at[g, c]
+    send(own_picks, own_picks, "ps", 0, (sib, g))
+
+    def picks_out(k, to, source):
+        send(own_picks, own_picks, "ag", k, (t, to), start=False).start()
+
+    each_peer(picks_out)
+    send(r.hid.at[RIM : 2 * RIM], r.hid.at[RIM + ROWS :], "rim", 4, (t, behind))
+    send(r.hid.at[ROWS : ROWS + RIM], r.hid.at[:RIM], "rim", 5, (t, ahead))
+
+    arrived(r.pickall.at[g, 1 - c], "ps", 0)
+    rows32 = r.pickall[g].reshape(32, 2 * HID)
+
+    def node_grads(rows):
+        return dot_nt(rows[:, :HID], r.sf[...]) + dot_nt(rows[:, HID:], r.nf[...])
+
+    node_grad = node_grads(rows32)
     r.nodeg[...] = node_grad
     for i in range(4):
         r.ngrad[i : i + 1, :] = r.nodeg[pl.ds(t * 4 + i, 1), :]
+    hand("ngrad")
     small = (node_grad * (1.0 / SEQ)).astype(BF16)
     r.act[...] = dot_nt(small, r.wo[...])
 
@@ -483,27 +581,60 @@
     norm_all = r.normed[...].reshape(NT * 256, D)
     for i in range(3):
         cols = slice(i * 128, (i + 1) * 128)
-        r.gfull[0, cols, :] = dot_tn(pre_all[:, cols], norm_all) * TEXT_SCALE
-    a_high, a_low = split(r.asum[...])
-    r.gfull[1] = (dot_tn(a_high, small) + dot_tn(a_low, small)) * TEXT_SCALE
+        r.gfull[cols, :] = dot_tn(pre_all[:, cols], norm_all) * TEXT_SCALE
 
     def pack(k, carry):
         rows = pl.ds(pl.multiple_of(k * OWN, 8), OWN)
-        both = jnp.concatenate([r.gfull[0, rows, :], r.gfull[1, rows, :]], axis=0)
-        r.gpack[k] = both.astype(BF16)
+        r.gpack[k] = halves(r.gfull[rows, :]).astype(BF16)
         return carry
 
     lax.fori_loop(0, NG, pack, 0)
     r.grecv[g] = r.gpack[g]
     scatter(lambda to: r.gpack.at[to], r.grecv, "gr")
 
-    for step in (1, 2, 3):
-        arrived(r.wgy.at[lax.rem(y + 4 - step, 4)], "a2", step)
-    quarter = r.wgy[0].astype(F32) + r.wgy[1].astype(F32)
-    quarter = quarter + r.wgy[2].astype(F32) + r.wgy[3].astype(F32)
-    r.wg2[...] = quarter.astype(BF16)
-    r.wgg[g] = r.wg2[g]
-    scatter(lambda to: r.wg2.at[to], r.wgg, "a3")
+    scatter_wait(r.l2, "l2")
+    r.l3[y] = over_peers(r.l2).astype(BF16)
+    for step, peer in ((1, up), (2, opp), (3, down)):
+        send(r.l3.at[y], r.l3.at[y], "l3", step, (peer, g))
+    for step in (1, 2, 3):
+        arrived(r.e2.at[lax.rem(y + 4 - step, 4)], "e2", step)
+    r.e3out[...] = over_y(r.e2).astype(BF16)
+
+    def piece_out(k, to, source):
+        @pl.when(to < 10)
+        def _():
+            send(r.e3out.at[pl.ds(to * 2, 2)], r.e3.at[g], "e3", k, (t, to), start=False).start()
+
+    each_peer(piece_out)
+
+    def picks_on(k, to, source):
+        ref = r.pickall.at[source, c]
+        arrived(ref, "ag", k)
+        send(ref, ref, "as", k, (sib, g), start=False).start()
+
+    each_peer(picks_on)
+
+    for step in (1, 2, 3):
+        arrived(r.l3.at[lax.rem(y + 4 - step, 4)], "l3", step)
+    r.late[c, pl.ds(g * 3, 3)] = over_y(r.l3).astype(BF16)
+    own_late = r.late.at[c, pl.ds(g * 3, 3)]
+
+    def late_out(k, to, source):
+        send(own_late, own_late, "l4", k, (t, to), start=False).start()
+
+    each_peer(late_out)
+
+    @pl.when(g < 10)
+    def _():
+        r.e3[g] = r.e3out[pl.ds(g * 2, 2)]
+        scatter_wait(r.e3, "e3")
+        r.early[c, y, pl.ds(g * 2, 2)] = over_peers(r.e3).astype(BF16)
+        own = r.early.at[c, y, pl.ds(g * 2, 2)]
+
+        def early_out(k, to, source):
+            send(own, own, "e4", k, (t, to), start=False).start()
+
+        each_peer(early_out)
 
     arrived(r.hid.at[RIM + ROWS :], "rim", 4)
     arrived(r.hid.at[:RIM], "rim", 5)
@@ -514,71 +645,134 @@
         rows = slice(i * 256, (i + 1) * 256)
         ext = slice(RIM + i * 256, RIM + (i + 1) * 256)
         r.gnn[rows, :] = (dot(r.hid[ext, :], r.ss[...]) + dot(r.e[rows, :], r.proj2[...])).astype(BF16)
-
-    scatter_wait(r.wgg, "a3")
-    piece = r.wgg[0].astype(F32)
-    for k in range(1, NG):
-        piece = piece + r.wgg[k].astype(F32)
-    r.wgall[c, y, g] = piece.astype(BF16)
-    own_piece = r.wgall.at[c, y, g]
-
-    def piece_out(k, to, source):
-        send(own_piece, own_piece, "a4", k, (t, to), start=False).start()
-
-    each_peer(piece_out)
+    hand("gnn")
+
+    each_peer(lambda k, to, source: arrived(r.late.at[c, pl.ds(source * 3, 3)], "l4", k))
+    send(r.late.at[c], r.late.at[c], "l5", 0, (sib, g))
+
+    def early_in(k, to, source):
+        @pl.when(source < 10)
+        def _():
+            arrived(r.early.at[c, y, pl.ds(source * 2, 2)], "e4", k)
+
+    each_peer(early_in)
+    own_quarter = r.early.at[c, y]
+    for step, peer in ((1, up), (3, down), (2, opp)):
+        send(own_quarter, own_quarter, "e5", step, (peer, g))
+
+    scatter_wait(r.acols, "ac")
+    each_peer(lambda k, to, source: arrived(r.pickall.at[source, 1 - c], "as", k))
+    small_all = (node_grads(r.pickall[...].reshape(NFT, 2 * HID)) * (1.0 / SEQ)).astype(BF16)
+    units = jnp.zeros((OWN, D), F32)
+    for q in range(4):
+        lanes = (r.acols[4 * q] + r.acols[4 * q + 1]) + (r.acols[4 * q + 2] + r.acols[4 * q + 3])
+        a_high, a_low = split(lanes)
+        block = small_all[q * 128 : (q + 1) * 128]
+        units = units + (dot(a_high, block) + dot(a_low, block))
+    r.gout[...] = units * TEXT_SCALE
+    hand("gout")
 
     scatter_wait(r.grecv, "gr")
-    summed = r.grecv[0].astype(F32)
-    for k in range(1, NG):
-        summed = summed + r.grecv[k].astype(F32)
-    r.gin[...] = summed[:OWN]
-    r.gout[...] = summed[OWN:]
-
-    each_peer(lambda k, to, source: arrived(r.wgall.at[c, y, source], "a4", k))
-    own_quarter = r.wgall.at[c, y]
-    for step, peer in ((1, up), (2, opp), (3, down)):
-        send(own_quarter, own_quarter, "a5", step, (peer, g))
-    for step in (1, 2, 3):
-        arrived(r.wgall.at[c, lax.rem(y + 4 - step, 4)], "a5", step)
-    own_side = r.wgall.at[c]
-    send(own_side, own_side, "a6", 0, (sib, g))
-    arrived(r.wgall.at[1 - c], "a6", 0)
-    for side, first, second in ((0, r.gsf, r.gss), (1, r.gnf, r.gns)):
-        for q in range(3):
-            first[q * 256 : (q + 1) * 256, :] = r.wgall[side, q].astype(F32).reshape(256, HID)
-        second[...] = r.wgall[side, 3].astype(F32).reshape(256, HID)
+    r.gin[...] = joined(over_peers(r.grecv))
+    hand("gin")
+
+    arrived(r.late.at[1 - c], "l5", 0)
+    hand("late")
+    for step in (1, 2, 3):
+        arrived(r.early.at[c, lax.rem(y + 4 - step, 4)], "e5", step)
+    send(r.early.at[c], r.early.at[c], "e6", 0, (sib, g))
+    arrived(r.early.at[1 - c], "e6", 0)
+    hand("early")
 
     for copy in pending:
         copy.wait_send()
-    scatter_sent(r.wpack.at[g], "w")
     scatter_sent(own_emb, "eg")
     each_peer(lambda k, to, source: send(own_emb, own_emb, "es", k, (sib, g), start=False).wait_send())
+    scatter_sent(r.acols.at[0], "ac")
     scatter_sent(r.pick1.at[0], "pg")
+    scatter_sent(own_picks, "ag")
+    each_peer(lambda k, to, source: send(own_picks, own_picks, "as", k, (sib, g), start=False).wait_send())
     scatter_sent(r.gpack.at[0], "gr")
-    scatter_sent(r.wg2.at[0], "a3")
-    scatter_sent(own_piece, "a4")
+    scatter_sent(r.l2.at[0], "l2")
+    scatter_sent(own_late, "l4")
+
+    def piece_sent(k, to, source):
+        @pl.when(to < 10)
+        def _():
+            send(r.e3.at[0], r.e3.at[0], "e3", k, (t, to), start=False).wait_send()
+
+    each_peer(piece_sent)
+
+    @pl.when(g < 10)
+    def _():
+        scatter_sent(r.e3.at[0], "e4")
+
+    for copy in handing:
+        copy.wait()
+
+
+def finish(fb, gnn, early, late, ngrad, gin, gout, sf, nf, gnn_o, tgrad, ngrad_o, gin_o, gout_o, gsf, gnf, gss, gns):
+    tgrad[...] = dot_nt(fb[:, :HID], sf[...]) + dot_nt(fb[:, HID:], nf[...])
+    gnn_o[...] = gnn[...]
+
+    @pl.when(pl.program_id(0) == 0)
+    def _():
+        ngrad_o[...] = ngrad[...]
+        gin_o[...] = gin[...]
+        gout_o[...] = gout[...]
+        for c in range(2):
+            cols = slice(c * 128, (c + 1) * 128)
+            gsf[:, cols] = early[c, :48].astype(F32).reshape(D, 128)
+            gss[:, cols] = early[c, 48:64].astype(F32).reshape(HID, 128)
+            gns[:, cols] = early[c, 64:].astype(F32).reshape(HID, 128)
+            gnf[:, cols] = late[c].astype(F32).reshape(D, 128)
 
 
 def per_device(states, w_in, w_out, table, adj, sources, node_ids, sf, nf, ss, ns, ups):
-    vmem = pl.BlockSpec(memory_space=pltpu.VMEM)
-    specs = [vmem] * len(INPUTS)
-    specs[INPUTS.index("src")] = pl.BlockSpec(memory_space=pltpu.SMEM)
-    scratch = [pltpu.VMEM(shape, dtype) for shape, dtype in SCRATCH.values()]
+    anywhere = pl.BlockSpec(memory_space=pl.ANY)
+    scratch = []
+    for kind in (INPUTS, HANDED, SCRATCH):
+        scratch += [pltpu.VMEM(shape, dtype) for shape, dtype in kind.values()]
     for count in SEMS.values():
         scratch += [pltpu.SemaphoreType.DMA((count,)), pltpu.SemaphoreType.DMA((count,))]
-    return pl.pallas_call(
+    scratch += [pltpu.SemaphoreType.DMA((len(INPUTS),)), pltpu.SemaphoreType.DMA((len(HANDED),))]
+    gnn, fb, early, late, ngrad, gin, gout = pl.pallas_call(
         body,
-        out_shape=tuple(jax.ShapeDtypeStruct(*spec) for spec in OUTPUTS.values()),
-        in_specs=specs,
-        out_specs=tuple([vmem] * len(OUTPUTS)),
+        out_shape=tuple(jax.ShapeDtypeStruct(*spec) for spec in HANDED.values()),
+        in_specs=[anywhere] * len(INPUTS),
+        out_specs=tuple([anywhere] * len(HANDED)),
         scratch_shapes=scratch,
         compiler_params=pltpu.CompilerParams(
             collective_id=0, has_side_effects=True, vmem_limit_bytes=62 * 1024 * 1024
         ),
     )(
-        states.reshape(4 * SEQ, D), w_in, w_out, table, adj.reshape(32, 128, 128),
-        sources, node_ids.reshape(1, NFT), sf, nf, ss, ns, ups,
+        states.reshape(4 * SEQ, D), w_in, w_out, node_ids.reshape(1, NFT), sources.T,
+        adj.reshape(32, 128, 128), ups, table, sf, nf, ss, ns,
     )
+
+    def whole(*shape):
+        return pl.BlockSpec(shape, lambda i: (0,) * len(shape))
+
+    def block(wide):
+        return pl.BlockSpec((256, wide), lambda i: (i, 0))
+
+    small = [whole(4, D), whole(OWN, D), whole(OWN, D)]
+    square = whole(HID, HID)
+    shapes = [
+        ((ROWS, HID), BF16), ((ROWS, D), F32), ((4, D), F32), ((OWN, D), F32), ((OWN, D), F32),
+        ((D, HID), F32), ((D, HID), F32), ((HID, HID), F32), ((HID, HID), F32),
+    ]
+    return tuple(pl.pallas_call(
+        finish,
+        grid=(4,),
+        out_shape=[jax.ShapeDtypeStruct(*shape) for shape in shapes],
+        in_specs=[
+            block(2 * HID), block(HID), whole(2, 80, 16, 128), whole(2, 48, 16, 128), *small,
+            whole(D, HID), whole(D, HID),
+        ],
+        out_specs=[block(HID), block(D), *small, whole(D, HID), whole(D, HID), square, square],
+        compiler_params=pltpu.CompilerParams(vmem_limit_bytes=62 * 1024 * 1024),
+    )(fb, gnn, early.reshape(2, 80, 16, 128), late, ngrad, gin, gout, sf, nf))
 
 
 def solution(mesh):

time: 134 us -> 104 us (0.78)
  Pallas kernels: 121 us -> 103 us
  local copies, waits for them, and re-layouts: 12.2 us -> 0 us
    pallas_call x1, Pallas kernels: 121 us -> 97.1 us  [per_device(): pl.pallas_call(body, out_shape=tuple((jax.ShapeDtypeStruct(*spec) for spe...]
    unnamed x24 -> x0, local copies, waits for them, and re-layouts: 12.2 us -> none
    pallas_call x0 -> x1, Pallas kernels: none -> 6.25 us  [per_device(): pl.pallas_call(finish, grid=(4,), out_shape=[jax.ShapeDtypeStruct(*shape)...]
where the time goes in v2:
time: 104 us
  Pallas kernels  103 us (99%)
    pallas_call x1, Pallas kernels, per_device(): pl.pallas_call(body, out_shape=tuple((jax.ShapeDtypeStruct(*spec) for spe...  97.1 us
    pallas_call x1, Pallas kernels, per_device(): pl.pallas_call(finish, grid=(4,), out_shape=[jax.ShapeDtypeStruct(*shape)...  6.25 us

profile of v2, /device:TPU:1, one launch (start us, length us, event | category | flops | bytes accessed | tf_op | source)
XLA Modules:
  0.0 104.2 jit_solution(10256212528272342624)
XLA Ops:
  0.6 97.1 %shard_map.187 = (bf16[1024,256]{1,0:T(8,128)(2,1)}, bf16[1024,512]{1,0:T(8,128)(2,1)}, bf16[2,4,20,16,128]{4,3,2,1,0:T(8,128)(2,1)}, bf16[2,48,16,128]{3,2,1,0:...) custom-call(bf16[256,768]{1,0:T(8,128)(2,1)} %bitcast.7, bf16[24,768]{1,0:T(8,128)(2,1)} %refs_1_.1, ...), custom_call_target="tpu_custom_call" | custom-call | tf_op jit(solution)/shard_map/pallas_call | solution.py:739
  97.8 6.3 %shard_map.188 = (bf16[1024,256]{1,0:T(8,128)(2,1)}, f32[1024,768]{1,0:T(8,128)}, f32[4,768]{1,0:T(4,128)}, f32[24,768]{1,0:T(8,128)}, f32[24,768]{1,0:T(8,128)}...) custom-call(bf16[1024,512]{1,0:T(8,128)(2,1)} %get-tuple-element.16.fb, ...), custom_call_target="tpu_custom_call" | custom-call | tf_op jit(solution)/shard_map/pallas_call | solution.py:765

commit v3 on v2

--- a/solution.py
+++ b/solution.py
@@ -114,7 +114,7 @@
     "grecv": ((NG, 2 * OWN, D // 2), BF16),
 }
 SEMS = {
-    "wi": 16, "wo": 16, "st": 9, "rim": 8, "pair": 1, "ye": 4, "eg": 16, "es": 16,
+    "wi": 16, "wo": 16, "st": 11, "rim": 8, "pair": 1, "ye": 4, "eg": 16, "es": 16,
     "ac": 16, "pk": 1, "pg": 16, "py": 4, "ps": 1, "ag": 16, "as": 16,
     "e1": 1, "e2": 4, "e3": 16, "e4": 16, "e5": 4, "e6": 1,
     "l1": 1, "l2": 16, "l3": 4, "l4": 16, "l5": 1, "gr": 16,
@@ -271,8 +271,11 @@
         send(own_out, own_out, "wo", step, (t, at_x(step) * 4 + z))
     mine = r.normed.at[t]
     send(mine, mine, "st", 0, (sib, g))
-    send(mine, mine, "st", 1, (up, g))
-    send(mine, mine, "st", 2, (down, g))
+    low_half, high_half = mine.at[:128], mine.at[128:]
+    send(low_half, low_half, "st", 1, (up, g))
+    send(high_half, high_half, "st", 2, (down, g))
+    send(high_half, high_half, "st", 9, (up, g))
+    send(low_half, low_half, "st", 10, (down, g))
 
     fetched("adj", "src")
     def tiles(b, carry):
@@ -335,6 +338,12 @@
         across = lax.broadcasted_iota(jnp.int32, (NFT, 128), 1).astype(F32) + start
         r.oht[:, e * 128 : (e + 1) * 128] = jnp.where(across == spot_col, 1.0, 0.0).astype(BF16)
 
+    from_down, from_up, far = r.normed.at[down], r.normed.at[up], r.normed.at[opp]
+    arrived(from_down.at[:128], "st", 1)
+    send(from_down.at[:128], from_down.at[:128], "st", 3, (up, g))
+    arrived(from_up.at[128:], "st", 2)
+    send(from_up.at[128:], from_up.at[128:], "st", 4, (down, g))
+
     def unpack(packed, out, place):
         def step(k, carry):
             rows = pl.ds(pl.multiple_of(k * OWN, 8), OWN)
@@ -364,29 +373,26 @@
         return slot + 1 - 2 * c
 
     encode(t)
-    from_down, from_up, far = r.normed.at[down], r.normed.at[up], r.normed.at[opp]
-    arrived(from_down, "st", 1)
-    send(from_down.at[:128], from_down.at[:128], "st", 3, (up, g))
-    send(from_down, from_down, "st", 5, (sib, g))
-    arrived(from_up, "st", 2)
-    send(from_up.at[128:], from_up.at[128:], "st", 4, (down, g))
-    send(from_up, from_up, "st", 6, (sib, g))
     arrived(r.normed.at[sib], "st", 0)
     encode(sib)
+    arrived(from_down.at[128:], "st", 9)
+    send(from_down, from_down, "st", 5, (sib, g))
+    arrived(from_up.at[:128], "st", 10)
+    send(from_up, from_up, "st", 6, (sib, g))
+    encode(down)
     send(r.tn.at[RIM : 2 * RIM], r.tn.at[RIM + ROWS :], "rim", 0, (t, behind))
     send(r.tn.at[ROWS : ROWS + RIM], r.tn.at[:RIM], "rim", 1, (t, ahead))
     r.b2out[0] = r.b2[:RIM, :].astype(BF16)
     r.b2out[1] = r.b2[RIM + ROWS :, :].astype(BF16)
     send(r.b2out.at[0], r.b2in.at[1], "rim", 2, (t, behind))
     send(r.b2out.at[1], r.b2in.at[0], "rim", 3, (t, ahead))
-    encode(down)
     encode(up)
+    arrived(r.normed.at[fellow(down)], "st", 5)
+    encode(fellow(down))
     arrived(far.at[:128], "st", 3)
     send(far.at[:128], far.at[:128], "st", 7, (sib, g))
     arrived(far.at[128:], "st", 4)
     send(far.at[128:], far.at[128:], "st", 8, (sib, g))
-    arrived(r.normed.at[fellow(down)], "st", 5)
-    encode(fellow(down))
     arrived(r.normed.at[fellow(up)], "st", 6)
     encode(fellow(up))
     encode(opp)
@@ -468,21 +474,14 @@
         value, slope = gelu_pair(pre)
         r.hid[ext, :] = value.astype(BF16)
         r.fb[rows, :HID] = (r.hg[rows, :] * slope).astype(BF16)
-    for i in (0, 5, 1, 2, 3, 4):
-        rows = slice(i * 256, (i + 1) * 256)
-        term = dot(r.et[rows, :], r.fb[:, :HID])
-        r.b1[rows, :] = term
-        r.b1b[rows, :] = term.astype(BF16)
-    send(r.b1b.at[:RIM], r.b1in.at[1], "rim", 6, (t, behind))
-    send(r.b1b.at[RIM + ROWS :], r.b1in.at[0], "rim", 7, (t, ahead))
-
-    for i in range(2):
-        rows = slice(i * 256, (i + 1) * 256)
-        first = dot(r.oht[rows, RIM : RIM + ROWS], r.fb[:, :HID]).astype(BF16)
-        back = dot(r.oht[rows, :], r.b1b[...]).astype(BF16)
-        r.pick[i, :, :, :HID] = first.reshape(NG, 16, HID)
-        r.pick[i, :, :, HID:] = back.reshape(NG, 16, HID)
-    send(r.pick.at[1 - c], r.pickin, "pk", 0, (sib, g))
+    def over_peers(ref):
+        total = ref[0].astype(F32)
+        for k in range(1, NG):
+            total = total + ref[k].astype(F32)
+        return total
+
+    def over_y(ref):
+        return (ref[0].astype(F32) + ref[1].astype(F32)) + (ref[2].astype(F32) + ref[3].astype(F32))
 
     def features(i):
         rows = slice(i * 256, (i + 1) * 256)
@@ -492,10 +491,6 @@
 
     for i in range(4):
         features(i)
-    arrived(r.pickin, "pk", 0)
-    r.pick1[...] = (r.pick[c].astype(F32) + r.pickin[...].astype(F32)).astype(BF16)
-    r.pickg[g] = r.pick1[g]
-    scatter(lambda to: r.pick1.at[to], r.pickg, "pg")
 
     def keep_grad(buffer, first, left, right):
         for q in range(left.shape[1] // 256):
@@ -511,38 +506,59 @@
     keep_grad(r.e0, 0, r.feat, r.fb[:, :HID])
     send(r.e0.at[1 - c], r.e1in, "e1", 0, (sib, g))
 
+    for i in (0, 5, 1, 2, 3, 4):
+        rows = slice(i * 256, (i + 1) * 256)
+        term = dot(r.et[rows, :], r.fb[:, :HID])
+        r.b1[rows, :] = term
+        r.b1b[rows, :] = term.astype(BF16)
+
+    for i in range(2):
+        rows = slice(i * 256, (i + 1) * 256)
+        first = dot(r.oht[rows, RIM : RIM + ROWS], r.fb[:, :HID]).astype(BF16)
+        back = dot(r.oht[rows, :], r.b1b[...]).astype(BF16)
+        r.pick[i, :, :, :HID] = first.reshape(NG, 16, HID)
+        r.pick[i, :, :, HID:] = back.reshape(NG, 16, HID)
+    send(r.pick.at[1 - c], r.pickin, "pk", 0, (sib, g))
+
+
+    arrived(r.e1in, "e1", 0)
+    r.e1[...] = (r.e0[c].astype(F32) + r.e1in[...].astype(F32)).astype(BF16)
+    r.e2[y] = r.e1[pl.ds(y * 20, 20)]
+    for step in (1, 3, 2):
+        to_y = lax.rem(y + step, 4)
+        send(r.e1.at[pl.ds(to_y * 20, 20)], r.e2.at[y], "e2", step, (to_y * 2 + c, g))
+    arrived(r.pickin, "pk", 0)
+    r.pick1[...] = (r.pick[c].astype(F32) + r.pickin[...].astype(F32)).astype(BF16)
+    r.pickg[g] = r.pick1[g]
+    scatter(lambda to: r.pick1.at[to], r.pickg, "pg")
+    send(r.b1b.at[:RIM], r.b1in.at[1], "rim", 6, (t, behind))
+    send(r.b1b.at[RIM + ROWS :], r.b1in.at[0], "rim", 7, (t, ahead))
+
+    scatter_wait(r.pickg, "pg")
+    r.picky[y] = over_peers(r.pickg).astype(BF16)
+    for step, peer in ((1, up), (2, opp), (3, down)):
+        send(r.picky.at[y], r.picky.at[y], "py", step, (peer, g))
+    for step in (1, 2, 3):
+        arrived(r.e2.at[lax.rem(y + 4 - step, 4)], "e2", step)
+    r.e3out[...] = over_y(r.e2).astype(BF16)
+
+    def piece_out(k, to, source):
+        @pl.when(to < 10)
+        def _():
+            send(r.e3out.at[pl.ds(to * 2, 2)], r.e3.at[g], "e3", k, (t, to), start=False).start()
+
+    each_peer(piece_out)
+
+
     arrived(r.b1in.at[0], "rim", 7)
     arrived(r.b1in.at[1], "rim", 6)
     r.b1[RIM : 2 * RIM, :] = r.b1[RIM : 2 * RIM, :] + r.b1in[0].astype(F32)
     r.b1[ROWS : ROWS + RIM, :] = r.b1[ROWS : ROWS + RIM, :] + r.b1in[1].astype(F32)
     r.fb[:, HID:] = r.b1[RIM : RIM + ROWS, :].astype(BF16)
     hand("fb")
-    arrived(r.e1in, "e1", 0)
-    r.e1[...] = (r.e0[c].astype(F32) + r.e1in[...].astype(F32)).astype(BF16)
-    r.e2[y] = r.e1[pl.ds(y * 20, 20)]
-    for step in (1, 3, 2):
-        to_y = lax.rem(y + step, 4)
-        send(r.e1.at[pl.ds(to_y * 20, 20)], r.e2.at[y], "e2", step, (to_y * 2 + c, g))
     keep_grad(r.l0, 0, r.feat, r.fb[:, HID:])
     send(r.l0.at[1 - c], r.l1in, "l1", 0, (sib, g))
 
-    def over_peers(ref):
-        total = ref[0].astype(F32)
-        for k in range(1, NG):
-            total = total + ref[k].astype(F32)
-        return total
-
-    def over_y(ref):
-        return (ref[0].astype(F32) + ref[1].astype(F32)) + (ref[2].astype(F32) + ref[3].astype(F32))
-
-    scatter_wait(r.pickg, "pg")
-    r.picky[y] = over_peers(r.pickg).astype(BF16)
-    for step, peer in ((1, up), (2, opp), (3, down)):
-        send(r.picky.at[y], r.picky.at[y], "py", step, (peer, g))
-    arrived(r.l1in, "l1", 0)
-    r.l1[...] = (r.l0[c].astype(F32) + r.l1in[...].astype(F32)).astype(BF16)
-    r.l2[g] = r.l1[pl.ds(g * 3, 3)]
-    scatter(lambda to: r.l1.at[pl.ds(to * 3, 3)], r.l2, "l2")
     for step in (1, 2, 3):
         arrived(r.picky.at[lax.rem(y + 4 - step, 4)], "py", step)
     r.pickall[g, c] = over_y(r.picky).astype(BF16)
@@ -553,6 +569,10 @@
         send(own_picks, own_picks, "ag", k, (t, to), start=False).start()
 
     each_peer(picks_out)
+    arrived(r.l1in, "l1", 0)
+    r.l1[...] = (r.l0[c].astype(F32) + r.l1in[...].astype(F32)).astype(BF16)
+    r.l2[g] = r.l1[pl.ds(g * 3, 3)]
+    scatter(lambda to: r.l1.at[pl.ds(to * 3, 3)], r.l2, "l2")
     send(r.hid.at[RIM : 2 * RIM], r.hid.at[RIM + ROWS :], "rim", 4, (t, behind))
     send(r.hid.at[ROWS : ROWS + RIM], r.hid.at[:RIM], "rim", 5, (t, ahead))
 
@@ -577,52 +597,6 @@
         return carry
 
     lax.fori_loop(0, 32, pre_grad, 0)
-    pre_all = r.pre[...].reshape(NT * 256, CHUNK)
-    norm_all = r.normed[...].reshape(NT * 256, D)
-    for i in range(3):
-        cols = slice(i * 128, (i + 1) * 128)
-        r.gfull[cols, :] = dot_tn(pre_all[:, cols], norm_all) * TEXT_SCALE
-
-    def pack(k, carry):
-        rows = pl.ds(pl.multiple_of(k * OWN, 8), OWN)
-        r.gpack[k] = halves(r.gfull[rows, :]).astype(BF16)
-        return carry
-
-    lax.fori_loop(0, NG, pack, 0)
-    r.grecv[g] = r.gpack[g]
-    scatter(lambda to: r.gpack.at[to], r.grecv, "gr")
-
-    scatter_wait(r.l2, "l2")
-    r.l3[y] = over_peers(r.l2).astype(BF16)
-    for step, peer in ((1, up), (2, opp), (3, down)):
-        send(r.l3.at[y], r.l3.at[y], "l3", step, (peer, g))
-    for step in (1, 2, 3):
-        arrived(r.e2.at[lax.rem(y + 4 - step, 4)], "e2", step)
-    r.e3out[...] = over_y(r.e2).astype(BF16)
-
-    def piece_out(k, to, source):
-        @pl.when(to < 10)
-        def _():
-            send(r.e3out.at[pl.ds(to * 2, 2)], r.e3.at[g], "e3", k, (t, to), start=False).start()
-
-    each_peer(piece_out)
-
-    def picks_on(k, to, source):
-        ref = r.pickall.at[source, c]
-        arrived(ref, "ag", k)
-        send(ref, ref, "as", k, (sib, g), start=False).start()
-
-    each_peer(picks_on)
-
-    for step in (1, 2, 3):
-        arrived(r.l3.at[lax.rem(y + 4 - step, 4)], "l3", step)
-    r.late[c, pl.ds(g * 3, 3)] = over_y(r.l3).astype(BF16)
-    own_late = r.late.at[c, pl.ds(g * 3, 3)]
-
-    def late_out(k, to, source):
-        send(own_late, own_late, "l4", k, (t, to), start=False).start()
-
-    each_peer(late_out)
 
     @pl.when(g < 10)
     def _():
@@ -636,19 +610,32 @@
 
         each_peer(early_out)
 
-    arrived(r.hid.at[RIM + ROWS :], "rim", 4)
-    arrived(r.hid.at[:RIM], "rim", 5)
-    for i in range(6):
-        rows = slice(i * 256, (i + 1) * 256)
-        r.proj2[rows, :] = dot(r.hid[rows, :], r.ns[...]).astype(BF16)
-    for i in range(4):
-        rows = slice(i * 256, (i + 1) * 256)
-        ext = slice(RIM + i * 256, RIM + (i + 1) * 256)
-        r.gnn[rows, :] = (dot(r.hid[ext, :], r.ss[...]) + dot(r.e[rows, :], r.proj2[...])).astype(BF16)
-    hand("gnn")
-
-    each_peer(lambda k, to, source: arrived(r.late.at[c, pl.ds(source * 3, 3)], "l4", k))
-    send(r.late.at[c], r.late.at[c], "l5", 0, (sib, g))
+    pre_all = r.pre[...].reshape(NT * 256, CHUNK)
+    norm_all = r.normed[...].reshape(NT * 256, D)
+    for i in range(3):
+        cols = slice(i * 128, (i + 1) * 128)
+        r.gfull[cols, :] = dot_tn(pre_all[:, cols], norm_all) * TEXT_SCALE
+
+    def pack(k, carry):
+        rows = pl.ds(pl.multiple_of(k * OWN, 8), OWN)
+        r.gpack[k] = halves(r.gfull[rows, :]).astype(BF16)
+        return carry
+
+    lax.fori_loop(0, NG, pack, 0)
+    r.grecv[g] = r.gpack[g]
+    scatter(lambda to: r.gpack.at[to], r.grecv, "gr")
+
+    scatter_wait(r.l2, "l2")
+    r.l3[y] = over_peers(r.l2).astype(BF16)
+    for step, peer in ((1, up), (2, opp), (3, down)):
+        send(r.l3.at[y], r.l3.at[y], "l3", step, (peer, g))
+
+    def picks_on(k, to, source):
+        ref = r.pickall.at[source, c]
+        arrived(ref, "ag", k)
+        send(ref, ref, "as", k, (sib, g), start=False).start()
+
+    each_peer(picks_on)
 
     def early_in(k, to, source):
         @pl.when(source < 10)
@@ -659,6 +646,29 @@
     own_quarter = r.early.at[c, y]
     for step, peer in ((1, up), (3, down), (2, opp)):
         send(own_quarter, own_quarter, "e5", step, (peer, g))
+
+    for step in (1, 2, 3):
+        arrived(r.l3.at[lax.rem(y + 4 - step, 4)], "l3", step)
+    r.late[c, pl.ds(g * 3, 3)] = over_y(r.l3).astype(BF16)
+    own_late = r.late.at[c, pl.ds(g * 3, 3)]
+
+    def late_out(k, to, source):
+        send(own_late, own_late, "l4", k, (t, to), start=False).start()
+
+    each_peer(late_out)
+
+
+    arrived(r.hid.at[RIM + ROWS :], "rim", 4)
+    arrived(r.hid.at[:RIM], "rim", 5)
+    for i in range(6):
+        rows = slice(i * 256, (i + 1) * 256)
+        r.proj2[rows, :] = dot(r.hid[rows, :], r.ns[...]).astype(BF16)
+    for i in range(4):
+        rows = slice(i * 256, (i + 1) * 256)
+        ext = slice(RIM + i * 256, RIM + (i + 1) * 256)
+        r.gnn[rows, :] = (dot(r.hid[ext, :], r.ss[...]) + dot(r.e[rows, :], r.proj2[...])).astype(BF16)
+    hand("gnn")
+
 
     scatter_wait(r.acols, "ac")
     each_peer(lambda k, to, source: arrived(r.pickall.at[source, 1 - c], "as", k))
@@ -672,15 +682,20 @@
     r.gout[...] = units * TEXT_SCALE
     hand("gout")
 
+
+    for step in (1, 2, 3):
+        arrived(r.early.at[c, lax.rem(y + 4 - step, 4)], "e5", step)
+    send(r.early.at[c], r.early.at[c], "e6", 0, (sib, g))
+    each_peer(lambda k, to, source: arrived(r.late.at[c, pl.ds(source * 3, 3)], "l4", k))
+    send(r.late.at[c], r.late.at[c], "l5", 0, (sib, g))
+
+
     scatter_wait(r.grecv, "gr")
     r.gin[...] = joined(over_peers(r.grecv))
     hand("gin")
 
     arrived(r.late.at[1 - c], "l5", 0)
     hand("late")
-    for step in (1, 2, 3):
-        arrived(r.early.at[c, lax.rem(y + 4 - step, 4)], "e5", step)
-    send(r.early.at[c], r.early.at[c], "e6", 0, (sib, g))
     arrived(r.early.at[1 - c], "e6", 0)
     hand("early")
 
@@ -711,21 +726,70 @@
         copy.wait()
 
 
-def finish(fb, gnn, early, late, ngrad, gin, gout, sf, nf, gnn_o, tgrad, ngrad_o, gin_o, gout_o, gsf, gnf, gss, gns):
-    tgrad[...] = dot_nt(fb[:, :HID], sf[...]) + dot_nt(fb[:, HID:], nf[...])
-    gnn_o[...] = gnn[...]
-
-    @pl.when(pl.program_id(0) == 0)
-    def _():
-        ngrad_o[...] = ngrad[...]
-        gin_o[...] = gin[...]
-        gout_o[...] = gout[...]
-        for c in range(2):
-            cols = slice(c * 128, (c + 1) * 128)
-            gsf[:, cols] = early[c, :48].astype(F32).reshape(D, 128)
-            gss[:, cols] = early[c, 48:64].astype(F32).reshape(HID, 128)
-            gns[:, cols] = early[c, 64:].astype(F32).reshape(HID, 128)
-            gnf[:, cols] = late[c].astype(F32).reshape(D, 128)
+FINISH = {
+    "fb": ((ROWS, 2 * HID), BF16),
+    "sf": ((D, HID), BF16),
+    "nf": ((D, HID), BF16),
+    "early": ((2, 80, 16, 128), BF16),
+    "late": ((2, 48, 16, 128), BF16),
+    "gnn": ((ROWS, HID), BF16),
+    "ngrad": ((4, D), F32),
+    "gin": ((OWN, D), F32),
+    "gout": ((OWN, D), F32),
+}
+RESULTS = {
+    "gnn": ((ROWS, HID), BF16),
+    "tgrad": ((ROWS, D), F32),
+    "ngrad": ((4, D), F32),
+    "gin": ((OWN, D), F32),
+    "gout": ((OWN, D), F32),
+    "gsf": ((D, HID), F32),
+    "gnf": ((D, HID), F32),
+    "gss": ((HID, HID), F32),
+    "gns": ((HID, HID), F32),
+}
+MADE = ("tgrad", "gsf", "gnf", "gss", "gns")
+
+
+def finish(*refs):
+    taken = iter(refs)
+    given = {name: next(taken) for name in FINISH}
+    out = {name: next(taken) for name in RESULTS}
+    r = SimpleNamespace(**{name: next(taken) for name in (*FINISH, *MADE)})
+    in_sems, out_sems = next(taken), next(taken)
+    leaving = []
+    fetches = {
+        name: pltpu.make_async_copy(given[name], getattr(r, name), in_sems.at[k])
+        for k, name in enumerate(FINISH)
+    }
+    for copy in fetches.values():
+        copy.start()
+    def leave(source, target, at):
+        copy = pltpu.make_async_copy(source, target, out_sems.at[at])
+        copy.start()
+        leaving.append(copy)
+
+    for name in ("fb", "sf", "nf"):
+        fetches[name].wait()
+    for i in range(4):
+        rows = slice(i * 256, (i + 1) * 256)
+        r.tgrad[rows, :] = dot_nt(r.fb[rows, :HID], r.sf[...]) + dot_nt(r.fb[rows, HID:], r.nf[...])
+        leave(r.tgrad.at[rows], out["tgrad"].at[rows], i)
+    for name in ("early", "late"):
+        fetches[name].wait()
+    for c in range(2):
+        cols = slice(c * 128, (c + 1) * 128)
+        r.gsf[:, cols] = r.early[c, :48].astype(F32).reshape(D, 128)
+        r.gss[:, cols] = r.early[c, 48:64].astype(F32).reshape(HID, 128)
+        r.gns[:, cols] = r.early[c, 64:].astype(F32).reshape(HID, 128)
+        r.gnf[:, cols] = r.late[c].astype(F32).reshape(D, 128)
+    for k, name in enumerate(MADE[1:]):
+        leave(getattr(r, name), out[name], 4 + k)
+    for k, name in enumerate(("gnn", "ngrad", "gin", "gout")):
+        fetches[name].wait()
+        leave(getattr(r, name), out[name], 8 + k)
+    for copy in leaving:
+        copy.wait()
 
 
 def per_device(states, w_in, w_out, table, adj, sources, node_ids, sf, nf, ss, ns, ups):
@@ -750,29 +814,17 @@
         adj.reshape(32, 128, 128), ups, table, sf, nf, ss, ns,
     )
 
-    def whole(*shape):
-        return pl.BlockSpec(shape, lambda i: (0,) * len(shape))
-
-    def block(wide):
-        return pl.BlockSpec((256, wide), lambda i: (i, 0))
-
-    small = [whole(4, D), whole(OWN, D), whole(OWN, D)]
-    square = whole(HID, HID)
-    shapes = [
-        ((ROWS, HID), BF16), ((ROWS, D), F32), ((4, D), F32), ((OWN, D), F32), ((OWN, D), F32),
-        ((D, HID), F32), ((D, HID), F32), ((HID, HID), F32), ((HID, HID), F32),
-    ]
+    scratch = [pltpu.VMEM(*spec) for spec in FINISH.values()]
+    scratch += [pltpu.VMEM(*RESULTS[name]) for name in MADE]
+    scratch += [pltpu.SemaphoreType.DMA((n,)) for n in (len(FINISH), 12)]
     return tuple(pl.pallas_call(
         finish,
-        grid=(4,),
-        out_shape=[jax.ShapeDtypeStruct(*shape) for shape in shapes],
-        in_specs=[
-            block(2 * HID), block(HID), whole(2, 80, 16, 128), whole(2, 48, 16, 128), *small,
-            whole(D, HID), whole(D, HID),
-        ],
-        out_specs=[block(HID), block(D), *small, whole(D, HID), whole(D, HID), square, square],
+        out_shape=[jax.ShapeDtypeStruct(*spec) for spec in RESULTS.values()],
+        in_specs=[anywhere] * len(FINISH),
+        out_specs=[anywhere] * len(RESULTS),
+        scratch_shapes=scratch,
         compiler_params=pltpu.CompilerParams(vmem_limit_bytes=62 * 1024 * 1024),
-    )(fb, gnn, early.reshape(2, 80, 16, 128), late, ngrad, gin, gout, sf, nf))
+    )(fb, sf, nf, early.reshape(2, 80, 16, 128), late, gnn, ngrad, gin, gout))
 
 
 def solution(mesh):

time: 104 us -> 95.1 us (0.914)
  Pallas kernels: 103 us -> 94.2 us
    pallas_call x1, Pallas kernels: 97.1 us -> 89.6 us  [per_device(): pl.pallas_call(body, out_shape=tuple((jax.ShapeDtypeStruct(*spec) for spe...]
    pallas_call x1, Pallas kernels: 6.25 us -> 4.62 us  [per_device(): pl.pallas_call(finish, out_shape=[jax.ShapeDtypeStruct(*spec) for spec in...]
where the time goes in v3:
time: 95.1 us; the launch traced here: 95 us
  Pallas kernels  94.2 us (99%)
    pallas_call x1, Pallas kernels, per_device(): pl.pallas_call(body, out_shape=tuple((jax.ShapeDtypeStruct(*spec) for spe...  89.6 us
    pallas_call x1, Pallas kernels, per_device(): pl.pallas_call(finish, out_shape=[jax.ShapeDtypeStruct(*spec) for spec in...  4.62 us

profile of v3, /device:TPU:1, one launch (start us, length us, event | category | flops | bytes accessed | tf_op | source)
XLA Modules:
  0.0 95.0 jit_solution(17017234519426142012)
XLA Ops:
  0.6 89.6 %shard_map.187 = (bf16[1024,256]{1,0:T(8,128)(2,1)}, bf16[1024,512]{1,0:T(8,128)(2,1)}, bf16[2,4,20,16,128]{4,3,2,1,0:T(8,128)(2,1)}, bf16[2,48,16,128]{3,2,1,0:...) custom-call(bf16[256,768]{1,0:T(8,128)(2,1)} %bitcast.7, bf16[24,768]{1,0:T(8,128)(2,1)} %refs_1_.2, ...), custom_call_target="tpu_custom_call" | custom-call | tf_op jit(solution)/shard_map/pallas_call | solution.py:803
  90.2 4.6 %shard_map.188 = (bf16[1024,256]{1,0:T(8,128)(2,1)}, f32[1024,768]{1,0:T(8,128)}, f32[4,768]{1,0:T(4,128)}, f32[24,768]{1,0:T(8,128)}, f32[24,768]{1,0:T(8,128)}...) custom-call(bf16[1024,512]{1,0:T(8,128)(2,1)} %get-tuple-element.16.refs_0_, ...), custom_call_target="tpu_custom_call" | custom-call | tf_op jit(solution)/shard_map/pallas_call | solution.py:820
